TPU v7x, 128 devices: a whole 4x4x4 slice. The times are simulated.
128 devices in a mesh: dp: 2 (over y_lo), seq: 4 (over y_hi, core), mp: 16 (over x, z).
Axes of the slice: x: 4, y: 4 (y_hi: 2, y_lo: 2; y = y_hi * 2 + y_lo), z: 4, core: 2. Of those that a mesh axis runs over, the one named last changes fastest.
Arguments:
- tokens: bfloat16 [2, 1024, 2048], P('dp', 'seq', 'mp'), may hold values from -6 to 6
- doc_lengths: int32 [2, 4], P('dp'), may hold values from 1 to 896, 1024 in all within a row
- cotangent: bfloat16 [2, 1024, 2048], P('dp', 'seq', 'mp'), may hold values from -6 to 6
- norm_gains: bfloat16 [2, 2048], P(None, 'mp'), may hold values from 0.099609375 to 1.8984375
- w_branch: bfloat16 [2, 2048, 2816], P(None, None, 'mp'), may hold values from -0.125 to 0.125
- conv_weight: float32 [4, 2816], P(None, 'mp'), may hold values from -3 to 3
- lru_bias: float32 [3, 2816], P(None, 'mp'), may hold values from -4 to 4
- decay: float32 [2816], P('mp'), may hold values from -11.6 to -3.4
- gate_weights: bfloat16 [2, 16, 176, 176], P(None, 'mp'), may hold values from -0.4375 to 0.4375
- w_out: bfloat16 [2816, 2048], P('mp'), may hold values from -0.21875 to 0.21875
- w_up: bfloat16 [2, 2048, 6144], P(None, None, 'mp'), may hold values from -0.125 to 0.125
- w_down: bfloat16 [6144, 2048], P('mp'), may hold values from -0.109375 to 0.109375
Outputs:
- block_out: bfloat16 [2, 1024, 2048], P('dp', 'seq', 'mp')
- grad_tokens: float32 [2, 1024, 2048], P('dp', 'seq', 'mp')
- grad_gains: float32 [2, 2048], P(None, 'mp')
- grad_branch: float32 [2, 2048, 2816], P(None, ('dp', 'seq'), 'mp')
- grad_conv_weight: float32 [4, 2816], P(None, 'mp')
- grad_bias: float32 [3, 2816], P(None, 'mp')
- grad_decay: float32 [2816], P('mp')
- grad_gates: float32 [2, 16, 176, 176], P(None, 'mp')
- grad_out: float32 [2816, 2048], P('mp', ('dp', 'seq'))
- grad_up: float32 [2, 2048, 6144], P(None, ('dp', 'seq'), 'mp')
- grad_down: float32 [6144, 2048], P('mp', ('dp', 'seq'))
- block_states: float32 [2, 4, 2816], P('dp', 'seq', 'mp')
Inputs may be any that keep to these rules, and one draw needn't show every extreme that they name: `doc_lengths`: each row's lengths sum to 1024, and each row has one document of exactly 896 tokens.
All inputs are finite; a program needn't handle non-finite values.
Results may differ from a plain program's by a relative error of at most 0.0096.
Values may be sent and summed in bfloat16 or wider, within the bound.
A program may use at most 128 MiB of HBM per device.

v0:
```python
from functools import partial

import jax
import jax.numpy as jnp
from jax import lax
from jax.sharding import PartitionSpec as P

eps = 1e-06


def passed_along(value, axis, steps):
    count = lax.axis_size(axis)
    initial, last = (max(0, -steps), min(count, count - steps))
    return lax.ppermute(value, axis, [(source, source + steps) for source in range(initial, last)])


def carried_in(array, axis, combine, identity, reverse):
    size, here = (lax.axis_size(axis), lax.axis_index(axis))
    everything = jax.tree.map(lambda part: lax.all_gather(part, axis), array)
    start = jax.tree.map(
        lambda part, zero: jnp.broadcast_to(jnp.asarray(zero, part.dtype), part.shape),
        array,
        identity,
    )

    def hop(k, before):
        at = size - 1 - k if reverse else k
        reached = at > here if reverse else at < here
        new = combine(before, jax.tree.map(lambda part: part[at], everything))
        return jax.tree.map(lambda a, b: jnp.where(reached, a, b), new, before)

    return lax.fori_loop(0, size, hop, start)


def combine(earlier, later):
    return (earlier[0] * later[0], later[0] * earlier[1] + later[1])


def lru_inputs(resets, pre, conv, decay):
    rate = jax.nn.softplus(decay)
    log_coef = -8.0 * jax.nn.sigmoid(pre[0]) * rate
    coef = jnp.exp(log_coef) * (1.0 - resets)[..., None]
    drive = jnp.sqrt(1.0 - jnp.exp(2.0 * log_coef) + 0.001) * jax.nn.sigmoid(pre[1]) * conv
    return (coef, drive)


def gated(left, right):
    return jax.nn.gelu(left) * right


def reduce_out(partial_sums):
    return lax.psum_scatter(partial_sums, "mp", scatter_dimension=2, tiled=True)


def norm_back(grad_part, full_in, scale, gain_full, gain_own):
    width = full_in.shape[2]
    cubed = scale * scale * scale
    grad_full = lax.psum(grad_part, "mp")
    weighted = grad_full * gain_full
    inner_sum = jnp.sum(weighted * full_in, axis=-1, keepdims=True)
    grad_in = scale * weighted - full_in * cubed * inner_sum / width
    grad_gain = jnp.sum(grad_full * full_in * scale, axis=(0, 1))
    own = gain_own.shape[0]
    start = lax.axis_index("mp") * own
    return (
        lax.dynamic_slice_in_dim(grad_in, start, own, 2),
        lax.dynamic_slice_in_dim(grad_gain, start, own, 0),
    )


def on_device(
    tokens,
    doc_lengths,
    cotangent,
    norm_gains,
    w_branch,
    conv_weight,
    lru_bias,
    decay,
    gate_weights,
    w_out,
    w_up,
    w_down,
):
    rows, span, own_width = tokens.shape
    channels = w_branch.shape[2]
    blocks_here = gate_weights.shape[1]
    block_width = gate_weights.shape[2]
    full_tokens, full_gains, full_cot = (
        lax.all_gather(tokens, "mp", axis=2, tiled=True),
        lax.all_gather(norm_gains, "mp", axis=1, tiled=True),
        lax.all_gather(cotangent, "mp", axis=2, tiled=True),
    )
    gains = full_gains.astype(jnp.float32)
    own_gains = norm_gains.astype(jnp.float32)
    starts = jnp.cumsum(doc_lengths, axis=1) - doc_lengths
    places = lax.axis_index("seq") * span + jnp.arange(-3, span, dtype=jnp.int32)
    segment = jnp.sum((places[None, :, None] >= starts[:, None, :]).astype(jnp.int32), axis=2)
    resets = jnp.any(places[None, 3:, None] == starts[:, None, :], axis=2).astype(jnp.float32)
    masks = [
        (segment[:, 3 - back : 3 - back + span] == segment[:, 3:]).astype(jnp.float32)[..., None]
        for back in (1, 2, 3)
    ]
    tokens_full = full_tokens.astype(jnp.float32)
    scale_one = lax.rsqrt(jnp.mean(tokens_full * tokens_full, axis=-1, keepdims=True) + eps)
    first = (tokens_full * scale_one * gains[0]).astype(jnp.bfloat16)
    proj = jnp.einsum("rld,kdc->krlc", first, w_branch, preferred_element_type=jnp.float32)
    inner = proj[1].astype(jnp.bfloat16)
    before = passed_along(inner[:, span - 3 :, :], "seq", 1)
    extended = jnp.concatenate([before, inner], axis=1).astype(jnp.float32)
    conv = lru_bias[0] + conv_weight[0] * extended[:, 3:]
    for back in (1, 2, 3):
        conv = conv + conv_weight[back] * masks[back - 1] * extended[:, 3 - back : 3 - back + span]
    conv_low = conv.astype(jnp.bfloat16)
    blocked = conv_low.reshape(rows, span, blocks_here, block_width)
    pre = jnp.einsum("rlnb,knbc->krlnc", blocked, gate_weights, preferred_element_type=jnp.float32)
    pre = pre.reshape(2, rows, span, channels) + lru_bias[1:, None, None, :]
    coef, drive = lru_inputs(resets, pre, conv, decay)
    through, local_state = lax.associative_scan(combine, (coef, drive), axis=1)
    identity = (jnp.ones((rows, channels), jnp.float32), jnp.zeros((rows, channels), jnp.float32))
    carried_coef, carried_state = carried_in(
        (through[:, -1], local_state[:, -1]), "seq", combine, identity, False
    )
    state = local_state + through * carried_state[:, None, :]
    mixed = gated(proj[0], state).astype(jnp.bfloat16)
    branch = reduce_out(jnp.einsum("rlc,cd->rld", mixed, w_out, preferred_element_type=jnp.float32))
    middle = tokens.astype(jnp.float32) + branch
    middle_low = middle.astype(jnp.bfloat16)
    middle_full = lax.all_gather(middle_low, "mp", axis=2, tiled=True).astype(jnp.float32)
    scale_two = lax.rsqrt(jnp.mean(middle_full * middle_full, axis=-1, keepdims=True) + eps)
    second = (middle_full * scale_two * gains[1]).astype(jnp.bfloat16)
    pair = jnp.einsum("rld,kdf->krlf", second, w_up, preferred_element_type=jnp.float32)
    hidden = gated(pair[0], pair[1]).astype(jnp.bfloat16)
    result = middle + reduce_out(
        jnp.einsum("rlf,fd->rld", hidden, w_down, preferred_element_type=jnp.float32)
    )
    block_out = result.astype(jnp.bfloat16)
    block_states = state[:, span - 1 :, :]
    grad_down = jnp.einsum("rlf,rld->fd", hidden, full_cot, preferred_element_type=jnp.float32)
    grad_hidden = jnp.einsum("rld,fd->rlf", full_cot, w_down, preferred_element_type=jnp.float32)
    _, hidden_back = jax.vjp(gated, pair[0], pair[1])
    grad_pair = jnp.stack(hidden_back(grad_hidden), 0).astype(jnp.bfloat16)
    grad_up = jnp.einsum("rld,krlf->kdf", second, grad_pair, preferred_element_type=jnp.float32)
    second_part = jnp.einsum("krlf,kdf->rld", grad_pair, w_up, preferred_element_type=jnp.float32)
    grad_mid_norm, gain_two = norm_back(second_part, middle_full, scale_two, gains[1], own_gains[1])
    grad_middle = cotangent.astype(jnp.float32) + grad_mid_norm
    grad_mid_full = lax.all_gather(grad_middle.astype(jnp.bfloat16), "mp", axis=2, tiled=True)
    grad_out = jnp.einsum("rlc,rld->cd", mixed, grad_mid_full, preferred_element_type=jnp.float32)
    grad_mixed = jnp.einsum("rld,cd->rlc", grad_mid_full, w_out, preferred_element_type=jnp.float32)
    _, mixed_back = jax.vjp(gated, proj[0], state)
    grad_y, grad_state = mixed_back(grad_mixed)
    next_coef = jnp.concatenate([coef[:, 1:], jnp.ones_like(coef[:, :1])], axis=1)
    reach, local_grad = lax.associative_scan(combine, (next_coef, grad_state), reverse=True, axis=1)
    summary = (through[:, -1], coef[:, 0] * local_grad[:, 0])
    carried_reach, incoming = carried_in(summary, "seq", combine, identity, True)
    grad_total = local_grad + reach * incoming[:, None, :]
    previous = jnp.concatenate([carried_state[:, None, :], state[:, :-1]], axis=1)
    _, lru_back = jax.vjp(partial(lru_inputs, resets), pre, conv, decay)
    grad_pre, conv_direct, grad_decay = lru_back((grad_total * previous, grad_total))
    grad_pre_low = grad_pre.astype(jnp.bfloat16)
    bias_gates = jnp.sum(grad_pre_low, axis=(1, 2), dtype=jnp.float32)
    grad_blocked = grad_pre_low.reshape(2, rows, span, blocks_here, block_width)
    grad_gates = jnp.einsum(
        "rlnb,krlnc->knbc", blocked, grad_blocked, preferred_element_type=jnp.float32
    )
    grad_conv = conv_direct + jnp.einsum(
        "krlnc,knbc->rlnb", grad_blocked, gate_weights, preferred_element_type=jnp.float32
    ).reshape(rows, span, channels)
    conv_grads = [jnp.sum(grad_conv * extended[:, 3:], axis=(0, 1))]
    grad_extended = jnp.pad(conv_weight[0] * grad_conv, ((0, 0), (3, 0), (0, 0)))
    for back in (1, 2, 3):
        weighted = masks[back - 1] * grad_conv
        conv_grads.append(jnp.sum(weighted * extended[:, 3 - back : 3 - back + span], axis=(0, 1)))
        grad_extended = grad_extended + jnp.pad(
            conv_weight[back] * weighted, ((0, 0), (3 - back, back), (0, 0))
        )
    conv_bias_grad = jnp.sum(grad_conv, axis=(0, 1))
    from_right = passed_along(grad_extended[:, :3], "seq", -1)
    grad_inner = grad_extended[:, 3:] + jnp.pad(from_right, ((0, 0), (span - 3, 0), (0, 0)))
    grad_proj = jnp.stack([grad_y, grad_inner], 0).astype(jnp.bfloat16)
    grad_branch = jnp.einsum("rld,krlc->kdc", first, grad_proj, preferred_element_type=jnp.float32)
    first_part = jnp.einsum(
        "krlc,kdc->rld", grad_proj, w_branch, preferred_element_type=jnp.float32
    )
    grad_in_norm, gain_one = norm_back(first_part, tokens_full, scale_one, gains[0], own_gains[0])
    grad_tokens = grad_middle + grad_in_norm
    large = (
        lax.psum_scatter(grad_branch, ("dp", "seq"), scatter_dimension=1, tiled=True),
        lax.psum_scatter(grad_out, ("dp", "seq"), scatter_dimension=1, tiled=True),
        lax.psum_scatter(grad_up, ("dp", "seq"), scatter_dimension=1, tiled=True),
        lax.psum_scatter(grad_down, ("dp", "seq"), scatter_dimension=1, tiled=True),
    )
    small = lax.psum(
        (
            jnp.stack([gain_one, gain_two], 0),
            jnp.stack(conv_grads, 0),
            jnp.concatenate([conv_bias_grad[None], bias_gates], 0),
            grad_decay,
            grad_gates,
        ),
        ("dp", "seq"),
    )
    return (
        block_out,
        grad_tokens,
        small[0],
        large[0],
        small[1],
        small[2],
        small[3],
        small[4],
        large[1],
        large[2],
        large[3],
        block_states,
    )


def solution(mesh):
    in_specs = (
        P("dp", "seq", "mp"),
        P("dp", None),
        P("dp", "seq", "mp"),
        P(None, "mp"),
        P(None, None, "mp"),
        P(None, "mp"),
        P(None, "mp"),
        P("mp"),
        P(None, "mp", None, None),
        P("mp", None),
        P(None, None, "mp"),
        P("mp", None),
    )
    out_specs = (
        P("dp", "seq", "mp"),
        P("dp", "seq", "mp"),
        P(None, "mp"),
        P(None, ("dp", "seq"), "mp"),
        P(None, "mp"),
        P(None, "mp"),
        P("mp"),
        P(None, "mp", None, None),
        P("mp", ("dp", "seq")),
        P(None, ("dp", "seq"), "mp"),
        P("mp", ("dp", "seq")),
        P("dp", "seq", "mp"),
    )
    return jax.shard_map(
        on_device, mesh=mesh, in_specs=in_specs, out_specs=out_specs, check_vma=False
    )
```

profile of v0, /device:TPU:1, one launch (start us, length us, event | category | flops | bytes accessed | tf_op | source)
XLA Modules:
  0.0 1179.7 jit_solution(1283043805503301177)
XLA Ops:
  9.7 18.7 %all_gather.27 = bf16[2,2048]{1,0:T(2,128)(2,1)S(1)} all-gather(bf16[2,128]{1,0:T(2,128)(2,1)} %param.19), channel_id=1, replica_groups=mesh['dp'=2,'seq'=4,'mp'=16] {'mp'}, dimensions={1}, use_global_device_ids=true | all-gather | bytes 8704 | tf_op jit(solution)/shard_map/all_gather | solution.py:91
  31.2 24.3 %all-gather.5.cloned.1.call-done = bf16[1,256,2048]{2,1,0:T(8,128)(2,1)} async-done(((bf16[1,256,128]{2,1,0:T(8,128)(2,1)}), bf16[1,256,2048]{2,1,0:T(8,128)(2,1)}) %all-gather.5.cloned.1.call-update) | async-done | bytes 1048592 | tf_op jit(solution)/shard_map/all_gather | solution.py:90
  60.7 6.6 collective-permute-start
  75.7 4.6 slice.619
  80.2 4.6 slice.618
  84.8 4.6 slice.617
  89.4 4.6 slice.621
  97.8 2.5 slice.625
  100.3 3.1 slice.622
  103.4 3.1 slice.623
  108.6 3.1 slice.627
  177.0 4.5 slice.673
  181.5 4.5 slice.616
  241.9 2.6 pad.232
  244.5 2.6 pad.233
  248.7 3.0 pad.235
  251.7 2.6 pad.249
  256.0 2.6 pad.248
  263.5 2.9 pad.234
  266.5 3.2 pad.251
  271.3 2.9 pad.250
  280.8 3.7 pad.252
  284.5 3.7 pad.253
  289.8 5.2 pad.255
  295.0 3.7 pad.237
  307.1 4.4 pad.254
  313.1 7.0 all_gather.28
  320.1 5.2 pad.239
  326.4 4.4 pad.238
  332.5 7.0 all_gather.29
  341.6 2.9 convolution_bitcast_fusion.2
  344.6 71.9 %reduce-scatter.7.cloned.1.call-done = f32[1,256,128]{2,1,0:T(8,128)} async-done(((f32[1,256,2048]{2,1,0:T(8,128)}), f32[1,256,128]{2,1,0:T(8,128)}) %reduce-scatter.7.cloned.1.call-update) | async-done | bytes 131088 | tf_op jit(solution)/shard_map/reduce_scatter | solution.py:52
  418.7 43.6 %all-gather.7.cloned.1.call-done = bf16[1,256,2048]{2,1,0:T(8,128)(2,1)} async-done(((bf16[1,256,128]{2,1,0:T(8,128)(2,1)}), bf16[1,256,2048]{2,1,0:T(8,128)(2,1)}) %all-gather.7.cloned.1.call-update) | async-done | bytes 1048592 | tf_op jit(solution)/shard_map/all_gather | solution.py:129
  465.0 3.1 convolution_bitcast_fusion.6
  468.2 39.2 %all-gather.9.cloned.1.call-done = bf16[1,256,2048]{2,1,0:T(8,128)(2,1)} async-done(((bf16[1,256,128]{2,1,0:T(8,128)(2,1)}), bf16[1,256,2048]{2,1,0:T(8,128)(2,1)}) %all-gather.9.cloned.1.call-update) | async-done | bytes 1048592 | tf_op jit(solution)/shard_map/all_gather | solution.py:92
  507.3 2.8 fusion.41
  516.1 87.3 %all-reduce.78.cloned.1.call-done = f32[1,256,2048]{2,1,0:T(8,128)} async-done(((f32[1,256,2048]{2,1,0:T(8,128)}), f32[1,256,2048]{2,1,0:T(8,128)}) %all-reduce.78.cloned.1.call-update) | async-done | bytes 2097168 | tf_op jit(solution)/shard_map/psum | solution.py:58
  603.3 2.7 multiply_reduce_fusion
  608.4 3.7 slice.696
  612.0 3.7 slice.705
  615.7 3.0 slice.698
  623.5 27.1 %all-gather.11.cloned.1.call-done = bf16[1,256,2048]{2,1,0:T(8,128)(2,1)} async-done(((bf16[1,256,128]{2,1,0:T(8,128)(2,1)}), bf16[1,256,2048]{2,1,0:T(8,128)(2,1)}) %all-gather.11.cloned.1.call-update) | async-done | bytes 1048592 | tf_op jit(solution)/shard_map/all_gather | solution.py:147
  653.1 3.0 slice.702
  656.1 3.0 slice.700
  688.5 3.7 slice.758
  713.1 3.0 pad.270
  716.1 3.0 pad.271
  720.2 3.0 pad.286
  723.2 3.0 pad.287
  726.9 8.6 all_gather.33
  737.7 3.8 convolution_bitcast_fusion.5
  745.3 5.0 collective-permute-done.1
  752.7 3.8 convolution_bitcast_fusion
  757.7 3.5 fusion.7
  761.3 2.8 fusion.3
  769.9 24.8 %all-reduce.82.cloned.1.call-done = f32[2,1,176,176]{2,3,0,1:T(8,128)} async-done(((f32[2,1,176,176]{2,3,0,1:T(8,128)}), f32[2,1,176,176]{2,3,0,1:T(8,128)}) %all-reduce.82.cloned.1.call-update) | async-done | bytes 247824 | tf_op jit(solution)/shard_map/psum | solution.py:193
  796.7 75.9 %reduce-scatter.9.cloned.1.call-done = f32[1,256,128]{2,1,0:T(8,128)} async-done(((f32[1,256,2048]{2,1,0:T(8,128)}), f32[1,256,128]{2,1,0:T(8,128)}) %reduce-scatter.9.cloned.1.call-update) | async-done | bytes 131088 | tf_op jit(solution)/shard_map/reduce_scatter | solution.py:52
  874.2 91.9 %all-reduce.80.cloned.1.call-done = f32[1,256,2048]{2,1,0:T(8,128)} async-done(((f32[1,256,2048]{2,1,0:T(8,128)}), f32[1,256,2048]{2,1,0:T(8,128)}) %all-reduce.80.cloned.1.call-update) | async-done | bytes 2097168 | tf_op jit(solution)/shard_map/psum | solution.py:58
  966.1 3.8 multiply_reduce_fusion.1
  969.9 30.9 %all-reduce.73 = (f32[2,128]{1,0:T(2,128)}, f32[4,176]{1,0:T(4,128)}, f32[3,176]{1,0:T(4,128)}, f32[176]{0:T(256)}) all-reduce(f32[2,128]{1,0:T(2,128)S(1)} %pad_maximum_fusion.35, f32[4,176]{1,0:T(4,128)S(1)} %pad_maximum_fusion.33, f32[3,176]{1,0:T(4,128)S(1)} %pad_maximum_fusion.34, ...), channel_id=1, replica_groups=mesh['dp'=2,'seq'=4,'mp'=16] {'dp','seq'}, use_global_device_ids=true, to_apply=%region_17.18 | all-reduce | flops 1664 | bytes 13312 | tf_op jit(solution)/shard_map/psum | solution.py:193
  1002.6 36.2 %reduce-scatter.15.cloned.1.call-done = f32[2,256,384]{1,2,0:T(8,128)} async-done(((f32[2,2048,384]{1,2,0:T(8,128)}), f32[2,256,384]{1,2,0:T(8,128)}) %reduce-scatter.15.cloned.1.call-update) | async-done | bytes 786448 | tf_op jit(solution)/shard_map/reduce_scatter | solution.py:190
  1041.1 46.7 %reduce-scatter.17.cloned.1.call-done = f32[384,256]{1,0:T(8,128)} async-done(((f32[384,2048]{1,0:T(8,128)}), f32[384,256]{1,0:T(8,128)}) %reduce-scatter.17.cloned.1.call-update) | async-done | bytes 393232 | tf_op jit(solution)/shard_map/reduce_scatter | solution.py:191
  1087.9 39.7 %reduce-scatter.13.cloned.1.call-done = f32[176,256]{1,0:T(8,128)} async-done(((f32[176,2048]{1,0:T(8,128)}), f32[176,256]{1,0:T(8,128)}) %reduce-scatter.13.cloned.1.call-update) | async-done | bytes 180240 | tf_op jit(solution)/shard_map/reduce_scatter | solution.py:189
  1127.5 45.2 %reduce-scatter.11.cloned.1.call-done = f32[2,256,176]{1,2,0:T(8,128)} async-done(((f32[2,2048,176]{1,2,0:T(8,128)}), f32[2,256,176]{1,2,0:T(8,128)}) %reduce-scatter.11.cloned.1.call-update) | async-done | bytes 360464 | tf_op jit(solution)/shard_map/reduce_scatter | solution.py:188
  (416 shorter events, 273.2 us)
Async XLA Ops:
  7.2 457.9 %copy-start = (bf16[2,2048,384]{2,1,0:T(8,128)(2,1)S(1)}, bf16[2,2048,384]{2,1,0:T(8,128)(2,1)}, u32[]{:S(2)}) copy-start(bf16[2,2048,384]{2,1,0:T(8,128)(2,1)} %param.26) | copy-start | bytes 9437188
  7.2 48.3 %all-gather.5.cloned.1.call-start = ((), (), s32[]{:S(2)}) async-start(), calls=%async_computation.6 | async-start | bytes 1114112 | tf_op jit(solution)/shard_map/all_gather | solution.py:90
  7.9 408.6 %reduce-scatter.7.cloned.1.call-start = ((), (), s32[]{:S(2)}) async-start(), calls=%async_computation.7 | async-start | bytes 2228224 | tf_op jit(solution)/shard_map/reduce_scatter | solution.py:52
  31.2 42.0 %copy-start.39 = (f32[1,176]{1,0:T(1,128)}, f32[1,176]{1,0:T(1,128)S(1)}, u32[]{:S(2)}) copy-start(f32[1,176]{1,0:T(1,128)S(1)} %get-tuple-element.470) | copy-start | bytes 2116
  57.0 10.9 copy-start.53
  57.0 11.5 copy-start.37
  57.6 10.3 copy-start.42
  60.7 8.5 collective-permute-start
  69.3 4.7 copy-start.51
  344.6 117.8 %all-gather.7.cloned.1.call-start = ((), (), s32[]{:S(2)}) async-start(), calls=%async_computation.8 | async-start | bytes 1114112 | tf_op jit(solution)/shard_map/all_gather | solution.py:129
  418.1 89.2 %all-gather.9.cloned.1.call-start = ((), (), s32[]{:S(2)}) async-start(), calls=%async_computation.10 | async-start | bytes 1114112 | tf_op jit(solution)/shard_map/all_gather | solution.py:92
  418.7 184.6 %all-reduce.78.cloned.1.call-start = ((), (), s32[]{:S(2)}) async-start(), calls=%async_computation.11 | async-start | bytes 4194304 | tf_op jit(solution)/shard_map/psum | solution.py:58
  513.3 90.1 %copy-start.45 = (f32[256]{0:T(256)S(1)}, f32[256]{0:T(256)}, u32[]{:S(2)}) copy-start(f32[256]{0:T(256)} %copy-done.44) | copy-start | bytes 3076
  513.3 137.4 %all-gather.11.cloned.1.call-start = ((), (), s32[]{:S(2)}) async-start(), calls=%async_computation.12 | async-start | bytes 1114112 | tf_op jit(solution)/shard_map/all_gather | solution.py:147
  516.0 90.0 %copy-start.36 = (bf16[1,256,128]{2,1,0:T(8,128)(2,1)S(1)}, bf16[1,256,128]{2,1,0:T(8,128)(2,1)}, u32[]{:S(2)}) copy-start(bf16[1,256,128]{2,1,0:T(8,128)(2,1)} %param.18) | copy-start | bytes 196612
  516.0 90.1 %copy-start.49 = (f32[256]{0:T(256)S(1)}, f32[256]{0:T(256)}, u32[]{:S(2)}) copy-start(f32[256]{0:T(256)} %get-tuple-element.477) | copy-start | bytes 3076
  516.1 92.2 %copy-start.6 = (f32[1,256,176]{1,2,0:T(8,128)S(1)}, f32[1,256,176]{1,2,0:T(8,128)}, u32[]{:S(2)}) copy-start(f32[1,256,176]{1,2,0:T(8,128)} %get-tuple-element.391) | copy-start | bytes 540676
  606.1 44.5 %copy-start.10 = (f32[1,256,176]{1,2,0:T(8,128)S(1)}, f32[1,256,176]{1,2,0:T(8,128)}, u32[]{:S(2)}) copy-start(f32[1,256,176]{1,2,0:T(8,128)} %get-tuple-element.385) | copy-start | bytes 540676
  606.1 44.5 %copy-start.16 = (bf16[176,2048]{1,0:T(8,128)(2,1)S(1)}, bf16[176,2048]{1,0:T(8,128)(2,1)}, u32[]{:S(2)}) copy-start(bf16[176,2048]{1,0:T(8,128)(2,1)} %param.25) | copy-start | bytes 2162692
  606.1 44.5 %copy-start.19 = (f32[256,352]{0,1:S(1)}, f32[256,352]{0,1}, u32[]{:S(2)}) copy-start(f32[256,352]{0,1} %copy-done.18) | copy-start | bytes 1081348
  608.0 186.8 %all-reduce.82.cloned.1.call-start = ((), (), s32[]{:S(2)}) async-start(), calls=%async_computation.15 | async-start | bytes 720896 | tf_op jit(solution)/shard_map/psum | solution.py:193
  608.4 44.7 %copy-start.20 = (f32[256,352]{0,1:S(1)}, f32[256,352]{0,1}, u32[]{:S(2)}) copy-start(f32[256,352]{0,1} %copy-done.18) | copy-start | bytes 1081348
  623.5 36.6 %copy-start.34 = (f32[1,128,176]{1,2,0:T(8,128)S(1)}, f32[1,128,176]{1,2,0:T(8,128)}, u32[]{:S(2)}) copy-start(f32[1,128,176]{1,2,0:T(8,128)} %slice.706) | copy-start | bytes 270340
  679.7 14.8 %copy-start.33 = (f32[1,1,176]{1,2,0:T(8,128)S(1)}, f32[1,1,176]{1,2,0:T(8,128)}, u32[]{:S(2)}) copy-start(f32[1,1,176]{1,2,0:T(8,128)} %get-tuple-element.412) | copy-start | bytes 2116
  694.0 3.3 copy-start.30
  696.7 3.2 copy-start.32
  698.3 4.1 copy-start.27
  698.3 4.1 copy-start.31
  700.9 6.7 copy-start.28
  700.9 6.7 copy-start.29
  702.3 7.0 copy-start.25
  702.5 10.3 copy-start.26
  705.7 7.3 copy-start.24
  712.9 22.7 %copy-start.5 = (f32[2,1,256,176]{2,3,1,0:T(8,128)S(1)}, f32[2,1,256,176]{2,3,1,0:T(8,128)}, u32[]{:S(2)}) copy-start(f32[2,1,256,176]{2,3,1,0:T(8,128)} %copy-done.4) | copy-start | bytes 1081348
  712.9 22.7 %copy-start.23 = (f32[1,1,176]{1,2,0:T(8,128)S(1)}, f32[1,1,176]{1,2,0:T(8,128)}, u32[]{:S(2)}) copy-start(f32[1,1,176]{1,2,0:T(8,128)} %copy.120) | copy-start | bytes 2116
  713.0 22.7 %copy-start.40 = (f32[1,176]{1,0:T(1,128)S(1)}, f32[1,176]{1,0:T(1,128)}, u32[]{:S(2)}) copy-start(f32[1,176]{1,0:T(1,128)} %copy-done.39) | copy-start | bytes 2116
  713.0 22.7 %copy-start.41 = (f32[1,176]{1,0:T(1,128)S(1)}, f32[1,176]{1,0:T(1,128)}, u32[]{:S(2)}) copy-start(f32[1,176]{1,0:T(1,128)} %get-tuple-element.471) | copy-start | bytes 2116
  713.0 22.7 %copy-start.46 = (f32[176]{0:T(256)S(1)}, f32[176]{0:T(256)}, u32[]{:S(2)}) copy-start(f32[176]{0:T(256)} %get-tuple-element.386) | copy-start | bytes 2116
  713.0 22.7 %copy-start.52 = (f32[256]{0:T(256)S(1)}, f32[256]{0:T(256)}, u32[]{:S(2)}) copy-start(f32[256]{0:T(256)} %convert_subtract_fusion) | copy-start | bytes 3076
  720.1 16.1 %copy-start.47 = (f32[176]{0:T(256)S(1)}, f32[176]{0:T(256)}, u32[]{:S(2)}) copy-start(f32[176]{0:T(256)} %get-tuple-element.387) | copy-start | bytes 2116
  726.9 9.7 copy-start.8
  737.6 3.9 copy-start.38
  737.6 135.0 %reduce-scatter.9.cloned.1.call-start = ((), (), s32[]{:S(2)}) async-start(), calls=%async_computation.9 | async-start | bytes 2228224 | tf_op jit(solution)/shard_map/reduce_scatter | solution.py:52
  741.5 9.0 copy-start.35
  741.5 224.6 %all-reduce.80.cloned.1.call-start = ((), (), s32[]{:S(2)}) async-start(), calls=%async_computation.13 | async-start | bytes 4194304 | tf_op jit(solution)/shard_map/psum | solution.py:58
  741.5 9.0 copy-start.9
  742.9 7.5 collective-permute-start.1
  750.5 2.1 copy-start.13
  750.5 2.1 copy-start.15
  752.6 286.2 %reduce-scatter.15.cloned.1.call-start = ((), (), s32[]{:S(2)}) async-start(), calls=%async_computation.17 | async-start | bytes 7077888 | tf_op jit(solution)/shard_map/reduce_scatter | solution.py:190
  756.5 1.2 copy-start.11
  756.5 331.4 %reduce-scatter.17.cloned.1.call-start = ((), (), s32[]{:S(2)}) async-start(), calls=%async_computation.18 | async-start | bytes 3538944 | tf_op jit(solution)/shard_map/reduce_scatter | solution.py:191
  761.2 3.0 copy-start.2
  761.2 3.0 copy-start.43
  761.3 366.3 %reduce-scatter.13.cloned.1.call-start = ((), (), s32[]{:S(2)}) async-start(), calls=%async_computation.16 | async-start | bytes 1622016 | tf_op jit(solution)/shard_map/reduce_scatter | solution.py:189
  764.1 408.6 %reduce-scatter.11.cloned.1.call-start = ((), (), s32[]{:S(2)}) async-start(), calls=%async_computation.14 | async-start | bytes 3244032 | tf_op jit(solution)/shard_map/reduce_scatter | solution.py:188
  766.6 3.3 copy-start.54
  766.6 3.3 copy-start.55
  766.6 3.3 copy-start.50
  766.6 106.0 %copy-start.17 = (bf16[1,256,128]{2,1,0:T(8,128)(2,1)S(1)}, bf16[1,256,128]{2,1,0:T(8,128)(2,1)}, u32[]{:S(2)}) copy-start(bf16[1,256,128]{2,1,0:T(8,128)(2,1)} %param.16) | copy-start | bytes 196612
  766.6 106.0 %copy-start.22 = (f32[1,256,128]{2,1,0:T(8,128)S(1)}, f32[1,256,128]{2,1,0:T(8,128)}, u32[]{:S(2)}) copy-start(f32[1,256,128]{2,1,0:T(8,128)} %reduce-scatter.7.cloned.1.call-done) | copy-start | bytes 393220
  874.2 126.6 %copy-start.21 = (f32[1,256,128]{2,1,0:T(8,128)S(1)}, f32[1,256,128]{2,1,0:T(8,128)}, u32[]{:S(2)}) copy-start(f32[1,256,128]{2,1,0:T(8,128)} %get-tuple-element.382) | copy-start | bytes 393220
  874.2 126.6 %copy-start.48 = (f32[256]{0:T(256)S(1)}, f32[256]{0:T(256)}, u32[]{:S(2)}) copy-start(f32[256]{0:T(256)} %get-tuple-element.475) | copy-start | bytes 3076
  966.0 206.7 %copy-start.1 = (bf16[2,2048,384]{2,1,0:T(8,128)(2,1)S(1)}, bf16[2,2048,384]{2,1,0:T(8,128)(2,1)}, u32[]{:S(2)}) copy-start(bf16[2,2048,384]{2,1,0:T(8,128)(2,1)} %param.26) | copy-start | bytes 9437188
  (7 other events, 5.9 us)
Sparse Core Ops, SparseCore 0:
  10.1 45.2 all-gather.4
  344.7 71.8 reduce-scatter.6
  419.5 42.8 all-gather.6
  464.6 42.7 all-gather.8
  513.4 89.9 all-reduce.77
  608.1 42.4 all-gather.10
  737.7 57.0 all-reduce.81
  798.4 74.1 reduce-scatter.8
  876.0 90.0 all-reduce.79
  968.4 70.3 reduce-scatter.14
  1042.0 45.8 reduce-scatter.16
  1090.8 36.6 reduce-scatter.12
  1130.7 41.9 reduce-scatter.10
where the time goes:
time: 1190 us; the launch traced here: 1180 us
  waiting for transfers between devices  660 us (55%)
  local copies, waits for them, and re-layouts  277 us (23%)
  other arithmetic  107 us (9%)
  blocking collectives  72.1 us (6%)
  matrix products  37.6 us (3%)
  between operations  15.9 us (1%)
    psum x2, waiting for transfers between devices, norm_back(): grad_full = lax.psum(grad_part, 'mp')  179 us
    reduce_scatter x2, waiting for transfers between devices, reduce_out(): return lax.psum_scatter(partial_sums, 'mp', scatter_dimension=2, tiled=True)  148 us
    slice x42, local copies, waits for them, and re-layouts, on_device(): through, local_state = lax.associative_scan(combine, (coef, drive), axis=1)  99.2 us
    pad x28, local copies, waits for them, and re-layouts, on_device(): through, local_state = lax.associative_scan(combine, (coef, drive), axis=1)  83.2 us
    slice x47, local copies, waits for them, and re-layouts, on_device(): lax.associative_scan(combine, (next_coef, grad_state), reverse=True, axis=1)  52.1 us
    reduce_scatter x1, waiting for transfers between devices, on_device(): lax.psum_scatter(grad_down, ('dp', 'seq'), scatter_dimension=1, tiled=True)  46.7 us
    reduce_scatter x1, waiting for transfers between devices, on_device(): lax.psum_scatter(grad_branch, ('dp', 'seq'), scatter_dimension=1, tiled=T...  45.2 us
    all_gather x1, waiting for transfers between devices, on_device(): lax.all_gather(middle_low, 'mp', axis=2, tiled=True).astype(jnp.float32)  43.6 us
  transfers between devices with their start and end apart: 15, of which 14 were waited for; matrix products, arithmetic and copies ran while one was open for 5% of the time, Pallas kernels for 0%

commit v1 on v0

v1 whole, which is shorter than its diff:
```python
import functools

import jax
import jax.numpy as jnp
from jax import lax
from jax.experimental import pallas as pl
from jax.experimental.pallas import tpu as pltpu
from jax.sharding import PartitionSpec as P

MESH = pl.DeviceIdType.MESH
f32, bf16 = jnp.float32, jnp.bfloat16

T, D, C, F, W = 256, 2048, 176, 384, 128
H = T // 2
EPS = 1e-06
N_SEMS = 288
Q = 16
ALPHA, CUBIC = 0.7978845608028654, 0.044715


def nn(a, b):
    return lax.dot_general(a, b, (((1,), (0,)), ((), ())), preferred_element_type=f32)


def nt(a, b):
    return lax.dot_general(a, b, (((1,), (1,)), ((), ())), preferred_element_type=f32)


def sigmoid(v):
    return 1.0 / (1.0 + jnp.exp(-v))


def gelu_both(v):
    square = v * v
    t = jnp.tanh(ALPHA * v * (1.0 + CUBIC * square))
    half = 0.5 * (1.0 + t)
    return v * half, half + 0.5 * v * (1.0 - t * t) * ALPHA * (1.0 + 3.0 * CUBIC * square)


def kernel(
    tokens, lengths, cot, gains, conv_w, bias, decay, hbm_branch, hbm_gates, hbm_out, hbm_up, hbm_down,
    o_block, o_tokens, o_gains, o_branch, o_conv, o_bias, o_decay, o_gates, o_out, o_up, o_down, o_states,
    w_branch, gates, w_out, w_up, w_down,
    tok_g, cot_g, mid_g, gm_g, first, second, cot_d, gm_d,
    part1, part2, part3, part4, rs_r1, rs_s2, rs_r2,
    ext, conv, aa, rr, ii, qq, coef, through, local, p0, p1, gel, dgel, state, prev, pad_a, pad_b, tp,
    pair, ghid, mid_own, gmid_own, scale1, scale2,
    g_down, g_up, g_out, g_branch, y_down, y_up, y_out, y_branch, r_pair,
    halo_s, halo_r, back_s, back_r, car_s, car_r, rev_s, rev_r,
    gg, gg_r, gg_y, gg_f, small, small_r, small_y,
    send_sems, recv_sems, copy_sems,
):
    me, seq, dp = lax.axis_index("mp"), lax.axis_index("seq"), lax.axis_index("dp")
    x, z = me // 4, me % 4
    core, y = seq % 2, (seq // 2) * 2 + dp

    def turn(value, by):
        return lax.rem(value + by + 4, 4)

    def on_x(d):
        return {"mp": turn(x, d) * 4 + z}

    def on_z(d):
        return {"mp": x * 4 + turn(z, d)}

    def on_y(d):
        there = turn(y, d)
        return {"dp": there % 2, "seq": (there // 2) * 2 + core}

    def on_seq(d):
        return {"seq": turn(seq, d)}

    other = {"seq": (seq // 2) * 2 + (1 - core)}

    count = [0]
    sent = []

    def send(src, dst, where):
        i = count[0]
        count[0] += 1
        copy = pltpu.make_async_remote_copy(
            src_ref=src, dst_ref=dst, send_sem=send_sems.at[i], recv_sem=recv_sems.at[i],
            device_id=where, device_id_type=MESH,
        )
        copy.start()
        sent.append(copy)
        return copy

    loads = []
    for i, (src, dst) in enumerate(
        ((hbm_branch, w_branch), (hbm_gates, gates), (hbm_out, w_out), (hbm_down, w_down), (hbm_up, w_up))
    ):
        load = pltpu.make_async_copy(src, dst, copy_sems.at[i])
        load.start()
        loads.append(load)

    barrier = pltpu.get_barrier_semaphore()
    partners = [on_x(d) for d in (1, 2, 3)] + [on_z(d) for d in (1, 2, 3)] + [on_y(d) for d in (1, 2, 3)]
    partners += [on_seq(d) for d in (1, 2, 3)]
    for where in partners:
        pl.semaphore_signal(barrier, inc=1, device_id=where, device_id_type=MESH)

    def axis_of(h, phase):
        return (on_x, on_z)[(h + phase) % 2]

    def place(h, first_hop, second_hop):
        if h == 0:
            return turn(x, -first_hop), turn(z, -second_hop)
        return turn(x, -second_hop), turn(z, -first_hop)

    ORDER = (1, 3, 2)

    def gather_start(buf, rows):
        arrivals = []

        def view(h, cx, cz):
            return buf.at[h, cx, cz, pl.ds(0, rows[h])]

        for d in ORDER:
            for h in range(2):
                ref = view(h, x, z)
                arrivals.append((h, d, send(ref, ref, axis_of(h, 0)(d))))
        last = []

        def pass_on(h, d):
            ref = view(h, *place(h, d, 0))
            for e in ORDER:
                last.append(send(ref, ref, axis_of(h, 1)(e)))

        for h in range(2):
            pass_on(h, 0)
        return arrivals, last, pass_on

    def gather_forward(gather):
        arrivals, _, pass_on = gather
        for h, d, copy in arrivals:
            copy.wait_recv()
            pass_on(h, d)

    def gather_end(gather):
        for copy in gather[1]:
            copy.wait_recv()

    def rider_tile(row):
        high = row.astype(bf16).astype(f32)
        index = lax.broadcasted_iota(jnp.int32, (Q, H), 0)
        return jnp.where(index == 0, high, jnp.where(index == 1, row - high, 0.0)).astype(bf16)

    def scatter_start(n, part, with_q):
        rows = 4 * H + (Q if with_q else 0)
        arrivals = []
        for d in (2, 1, 3):
            for h in range(2):
                there = turn((z, x)[h], d)
                src = part.at[h, there, pl.ds(0, rows)]
                arrivals.append(send(src, rs_r1.at[n, h, d - 1, pl.ds(0, rows)], axis_of(h, 1)(d)))
        return arrivals

    def scatter_middle(n, part, with_q, arrivals):
        rows = H + (Q if with_q else 0)
        for copy in arrivals:
            copy.wait_recv()
        last = []
        for h in range(2):
            mine = (z, x)[h]
            for c in range(4 + with_q):
                size = H if c < 4 else Q
                at = pl.ds(c * H, size)
                total = part[h, mine, at].astype(f32)
                for d in range(3):
                    total += rs_r1[n, h, d, at].astype(f32)
                if c < 4:
                    rs_s2[n, h, c, pl.ds(0, H)] = total.astype(bf16)
                else:
                    tile = rider_tile(jnp.sum(total, axis=0, keepdims=True))
                    for k in range(4):
                        rs_s2[n, h, k, pl.ds(H, Q)] = tile
        for d in (2, 1, 3):
            for h in range(2):
                there = turn((x, z)[h], d)
                src = rs_s2.at[n, h, there, pl.ds(0, rows)]
                last.append(send(src, rs_r2.at[n, h, d - 1, pl.ds(0, rows)], axis_of(h, 0)(d)))
        return last

    def scatter_end(n, with_q, last):
        for copy in last:
            copy.wait_recv()
        out, column = [], []
        for h in range(2):
            mine = (x, z)[h]
            total = rs_s2[n, h, mine, pl.ds(0, H)].astype(f32)
            for d in range(3):
                total += rs_r2[n, h, d, pl.ds(0, H)].astype(f32)
            out.append(total)
            if with_q:
                rider = rs_s2[n, h, mine, pl.ds(H, Q)].astype(f32)
                for d in range(3):
                    rider += rs_r2[n, h, d, pl.ds(H, Q)].astype(f32)
                row = jnp.sum(rider, axis=0, keepdims=True)
                column.append(jnp.broadcast_to(row, (H, H)).T)
        return jnp.concatenate(out, 0), (jnp.concatenate(column, 0) if with_q else None)

    def put_part(part, block, value):
        low = value.astype(bf16)
        for half_block in range(2):
            c = 2 * block + half_block
            cx, cz = c // 4, c % 4
            piece = low[:, half_block * W : (half_block + 1) * W]
            part[0, cz, pl.ds(cx * H, H)] = piece[:H]
            part[1, cx, pl.ds(cz * H, H)] = piece[H:]

    def put_rider(part, products):
        for h in range(2):
            row = jnp.sum(products[h * H : (h + 1) * H].T, axis=0, keepdims=True)
            tile = rider_tile(row)
            for t in range(4):
                part[h, t, pl.ds(4 * H, Q)] = tile

    def chunk(buf, c):
        return jnp.concatenate([buf[0, c // 4, c % 4, pl.ds(0, H)], buf[1, c // 4, c % 4, pl.ds(0, H)]], 0)

    def gain_row(k, c):
        return tok_g[0, c // 4, c % 4, pl.ds(H, Q)].astype(f32)[k : k + 1]

    def norm(buf, k, scale_ref, dst):
        total = jnp.zeros((T, W), f32)
        for c in range(16):
            v = chunk(buf, c).astype(f32)
            total += v * v
        scale = lax.rsqrt(jnp.sum(total, axis=1, keepdims=True) * (1.0 / D) + EPS)
        scale_ref[...] = jnp.broadcast_to(scale, (T, W))
        for c in range(16):
            v = chunk(buf, c).astype(f32)
            dst[:, c * W : (c + 1) * W] = (v * scale_ref[...] * gain_row(k, c)).astype(bf16)

    def dense(buf, dst):
        for c in range(16):
            dst[:, c * W : (c + 1) * W] = chunk(buf, c)

    def grad_start(g, rows, left, right):
        for there in range(4):
            for core_there in range(2):
                j = (there % 2) * 4 + (there // 2) * 2 + core_there
                g[core_there, there, pl.ds(0, rows)] = nn(left, right[:, j * 256 : (j + 1) * 256]).astype(bf16)

    def grad_pair(g, r):
        return send(g.at[1 - core], r, other)

    def grad_middle(g, r, into, copy):
        copy.wait_recv()
        for there in range(4):
            g[core, there] = (g[core, there].astype(f32) + r[there].astype(f32)).astype(bf16)
        return [send(g.at[core, turn(y, d)], into.at[d - 1], on_y(d)) for d in (2, 1, 3)]

    def grad_end(g, into, copies, at):
        for copy in copies:
            copy.wait_recv()
        total = g[core, y, at].astype(f32)
        for d in range(3):
            total += into[d, at].astype(f32)
        return total

    def transposed(value):
        tp[:, :C] = value
        return tp[...].T[:C]

    gain_tile = jnp.concatenate([gains[...].astype(f32), jnp.zeros((Q - 2, W), f32)], 0).astype(bf16)
    for h in range(2):
        tok_g[h, x, z, pl.ds(0, H)] = tokens[pl.ds(h * H, H)]
        cot_g[h, x, z] = cot[pl.ds(h * H, H)]
    tok_g[0, x, z, pl.ds(H, Q)] = gain_tile
    tp[...] = jnp.zeros_like(tp)
    pl.semaphore_wait(barrier, len(partners))
    tok_gather = gather_start(tok_g, (H + Q, H))
    gather_forward(tok_gather)
    cot_gather = gather_start(cot_g, (H, H))

    row = lax.broadcasted_iota(jnp.int32, (T, 1), 0)
    place_here = row + seq * T
    start, begins = 0, [0]
    for j in range(3):
        start = start + lengths[0, j]
        begins.append(start)

    def begin_at(p):
        hit = p == begins[0]
        for b in begins[1:]:
            hit = jnp.logical_or(hit, p == b)
        return hit

    fresh = [begin_at(place_here - k) for k in range(3)]
    not_reset = jnp.where(fresh[0], 0.0, 1.0)
    masks = [not_reset]
    for k in (1, 2):
        masks.append(masks[-1] * jnp.where(fresh[k], 0.0, 1.0))

    gather_end(tok_gather)
    norm(tok_g, 0, scale1, first)
    for load in loads[:2]:
        load.wait()

    value = nn(first[...], w_branch[1])
    p1[...] = value
    inner = value.astype(bf16).astype(f32)
    ext[pl.ds(8, T)] = inner
    halo_s[:, :C] = inner[T - 8 :]
    halo = send(halo_s, halo_r, on_seq(1))
    value = nn(first[...], w_branch[0])
    p0[...] = value
    act, slope = gelu_both(value)
    gel[...] = act
    dgel[...] = slope
    gather_forward(cot_gather)
    halo.wait_recv()
    ext[pl.ds(0, 8)] = halo_r[:, :C]
    total = bias[0:1] + conv_w[0:1] * ext[pl.ds(8, T)]
    for k in (1, 2, 3):
        total = total + conv_w[k : k + 1] * (masks[k - 1] * ext[pl.ds(8 - k, T)])
    conv[...] = total
    conv_low = total.astype(bf16)
    rate = jax.nn.softplus(decay[...])
    r_gate = sigmoid(nn(conv_low, gates[0, 0]) + bias[1:2])
    rr[...] = r_gate
    a = jnp.exp(-8.0 * r_gate * rate)
    aa[...] = a
    coef[...] = a * not_reset
    i_gate = sigmoid(nn(conv_low, gates[1, 0]) + bias[2:3])
    ii[...] = i_gate
    root = jnp.sqrt(1.0 - a * a + 0.001)
    qq[...] = root

    def scan(A, B, reverse):
        step = 1
        while step < T:
            for ref, v, fill in ((pad_a, A, 1.0), (pad_b, B, 0.0)):
                ref[pl.ds(H, T)] = v
                ref[pl.ds(H + T if reverse else 0, H)] = jnp.full((H, C), fill, f32)
            at = pl.ds(H + step if reverse else H - step, T)
            B = B + A * pad_b[at]
            A = A * pad_a[at]
            step *= 2
        return A, B

    A, B = scan(coef[...], root * i_gate * conv[...], False)
    through[...] = A
    local[...] = B
    car_s[0:1, :C] = A[T - 1 :]
    car_s[1:2, :C] = B[T - 1 :]
    carries = [send(car_s, car_r.at[d - 1], on_seq(d)) for d in (1, 2, 3)]
    gather_end(cot_gather)
    dense(cot_g, cot_d)
    for load in loads[2:]:
        load.wait()
    ghid[...] = nt(cot_d[...], w_down[...])
    for copy in carries:
        copy.wait_recv()

    def fold(got, own, reverse):
        carried = jnp.zeros((1, C), f32)
        for d in (3, 2, 1):
            here = (seq + d < 4) if reverse else (seq - d >= 0)
            slot = 4 - d if reverse else d
            new = got[slot - 1, 0:1, :C] * carried + got[slot - 1, 1:2, :C]
            carried = jnp.where(here, new, carried)
        return carried

    carried = fold(car_r, car_s, False)
    value = local[...] + through[...] * carried
    state[...] = value
    prev[pl.ds(8, T)] = value
    prev[7:8] = carried
    o_states[...] = value[T - 1 :]
    mixed = gel[...] * value
    mixed_low = mixed.astype(bf16)
    for j in range(8):
        put_part(part1, j, nn(mixed_low, w_out[:, j * 256 : (j + 1) * 256]))
    arrivals = scatter_start(0, part1, False)
    mixed_t = transposed(mixed).astype(bf16)
    last = scatter_middle(0, part1, False, arrivals)
    branch, _ = scatter_end(0, False, last)
    middle = tokens[...].astype(f32) + branch
    mid_own[...] = middle
    middle_low = middle.astype(bf16)
    for h in range(2):
        mid_g[h, x, z] = middle_low[h * H : (h + 1) * H]
    mid_gather = gather_start(mid_g, (H, H))
    gather_forward(mid_gather)
    gather_end(mid_gather)
    norm(mid_g, 1, scale2, second)

    pair0 = nn(second[...], w_up[0])
    pair1 = nn(second[...], w_up[1])
    act, slope = gelu_both(pair0)
    hidden = act * pair1
    gh = ghid[...]
    gp0 = slope * pair1 * gh
    gp1 = act * gh
    products = gp0 * pair0 + gp1 * pair1
    products = products[:, :W] + products[:, W : 2 * W] + products[:, 2 * W :]
    put_rider(part2, products)
    gp0_low, gp1_low = gp0.astype(bf16), gp1.astype(bf16)
    for j in range(8):
        at = slice(j * 256, (j + 1) * 256)
        put_part(part2, j, nt(gp0_low, w_up[0, at]) + nt(gp1_low, w_up[1, at]))
    arrivals = scatter_start(1, part2, True)
    hidden_low = hidden.astype(bf16)
    for j in range(8):
        put_part(part3, j, nn(hidden_low, w_down[:, j * 256 : (j + 1) * 256]))
    grad_start(g_down, F, hidden.T.astype(bf16), cot_d)
    down_pair = grad_pair(g_down, r_pair.at[:, pl.ds(0, F)])
    last = scatter_middle(1, part2, True, arrivals)
    for k, gp in ((0, gp0), (1, gp1)):
        left = gp.T.astype(bf16)
        for there in range(4):
            for core_there in range(2):
                j = (there % 2) * 4 + (there // 2) * 2 + core_there
                g_up[core_there, there, pl.ds(k * F, F)] = nn(
                    left, second[:, j * 256 : (j + 1) * 256]
                ).astype(bf16)
    up_pair = grad_pair(g_up, r_pair.at[:, pl.ds(F, 2 * F)])
    down_y = grad_middle(g_down, r_pair.at[:, pl.ds(0, F)], y_down, down_pair)

    grad_n, q = scatter_end(1, True, last)
    v = mid_own[...].astype(bf16).astype(f32)
    s = scale2[...]
    gain = gains[1:2].astype(f32)
    grad_middle_own = cot[...].astype(f32) + s * gain * grad_n - v * s * s * q * (1.0 / D)
    gmid_own[...] = grad_middle_own
    small[...] = jnp.zeros_like(small)
    small[1:2, :W] = jnp.sum(grad_n * v * s, axis=0, keepdims=True)
    low = grad_middle_own.astype(bf16)
    for h in range(2):
        gm_g[h, x, z] = low[h * H : (h + 1) * H]
    gm_gather = gather_start(gm_g, (H, H))
    up_y = grad_middle(g_up, r_pair.at[:, pl.ds(F, 2 * F)], y_up, up_pair)
    gather_forward(gm_gather)
    gather_end(gm_gather)
    out_arrivals = scatter_start(2, part3, False)
    dense(gm_g, gm_d)

    grad_mixed = nt(gm_d[...], w_out[...])
    grad_y = dgel[...] * state[...] * grad_mixed
    grad_state = gel[...] * grad_mixed
    pad_a[pl.ds(0, T)] = coef[...]
    pad_a[pl.ds(T, 8)] = jnp.ones((8, C), f32)
    A, B = scan(pad_a[pl.ds(1, T)], grad_state, True)
    rev_s[0:1, :C] = through[T - 1 :]
    rev_s[1:2, :C] = coef[0:1] * B[0:1]
    carries = [send(rev_s, rev_r.at[d - 1], on_seq(d)) for d in (1, 2, 3)]
    grad_start(g_out, C, mixed_t, gm_d)
    out_pair = grad_pair(g_out, r_pair.at[:, pl.ds(3 * F, C)])
    for copy in carries:
        copy.wait_recv()
    total = B + A * fold(rev_r, rev_s, True)
    a, r_gate, i_gate, root, cv = aa[...], rr[...], ii[...], qq[...], conv[...]
    t_i = total * i_gate
    d_log = total * prev[pl.ds(7, T)] * coef[...] - t_i * cv * (a * a / root)
    d_gate = d_log * r_gate
    small[9:10, :C] = -8.0 * sigmoid(decay[...]) * jnp.sum(d_gate, axis=0, keepdims=True)
    gpre0 = -8.0 * rate * d_gate * (1.0 - r_gate)
    direct = t_i * root
    gpre1 = direct * cv * (1.0 - i_gate)
    low0, low1 = gpre0.astype(bf16), gpre1.astype(bf16)
    small[7:8, :C] = jnp.sum(low0.astype(f32), axis=0, keepdims=True)
    small[8:9, :C] = jnp.sum(low1.astype(f32), axis=0, keepdims=True)
    grad_conv = direct + nt(low0, gates[0, 0]) + nt(low1, gates[1, 0])
    small[6:7, :C] = jnp.sum(grad_conv, axis=0, keepdims=True)
    edge = jnp.zeros((8, C), f32)
    grad_inner = jnp.zeros((T, C), f32)
    for k in range(4):
        weighted = grad_conv if k == 0 else masks[k - 1] * grad_conv
        small[2 + k : 3 + k, :C] = jnp.sum(weighted * ext[pl.ds(8 - k, T)], axis=0, keepdims=True)
        if k == 0:
            pad_a[pl.ds(0, 8)] = jnp.zeros((8, C), f32)
            pad_a[pl.ds(8 + T, 8)] = jnp.zeros((8, C), f32)
        pad_a[pl.ds(8, T)] = conv_w[k : k + 1] * weighted
        edge += pad_a[pl.ds(k, 8)]
        grad_inner += pad_a[pl.ds(8 + k, T)]
    back_s[:, :C] = edge
    back = send(back_s, back_r, on_seq(-1))
    cv_t = transposed(cv).astype(bf16)
    gg[0, :, :C] = nn(cv_t, low0).astype(bf16)
    gg[1, :, :C] = nn(cv_t, low1).astype(bf16)
    gg_pair = send(gg.at[1 - core], gg_r, other)
    out_last = scatter_middle(2, part3, False, out_arrivals)
    out_y = grad_middle(g_out, r_pair.at[:, pl.ds(3 * F, C)], y_out, out_pair)
    gy_t = transposed(grad_y).astype(bf16)
    grad_start(g_branch.at[0], C, gy_t, first)
    back.wait_recv()
    ext[pl.ds(0, T)] = grad_inner
    ext[pl.ds(T - 8, 8)] = grad_inner[T - 8 :] + back_r[:, :C]
    grad_inner = ext[pl.ds(0, T)]
    gpr0, gpr1 = grad_y.astype(bf16), grad_inner.astype(bf16)
    tp[:, :C] = grad_y * p0[...] + grad_inner * p1[...]
    put_rider(part4, tp[:, :W] + tp[:, W:])
    for j in range(8):
        at = slice(j * 256, (j + 1) * 256)
        put_part(part4, j, nt(gpr0, w_branch[0, at]) + nt(gpr1, w_branch[1, at]))
    arrivals = scatter_start(3, part4, True)
    gi_t = transposed(grad_inner).astype(bf16)
    grad_start(g_branch.at[1], C, gi_t, first)
    b0_pair = send(g_branch.at[0, 1 - core], r_pair.at[:, pl.ds(3 * F + C, C)], other)
    b1_pair = send(g_branch.at[1, 1 - core], r_pair.at[:, pl.ds(3 * F + 2 * C, C)], other)
    gg_pair.wait_recv()
    gg_y[y] = (gg[core].astype(f32) + gg_r[...].astype(f32)).astype(bf16)
    gg_copies = [send(gg_y.at[y], gg_y.at[y], on_y(d)) for d in (2, 1, 3)]
    last = scatter_middle(3, part4, True, arrivals)
    b0_y = grad_middle(g_branch.at[0], r_pair.at[:, pl.ds(3 * F + C, C)], y_branch.at[0], b0_pair)
    b1_y = grad_middle(g_branch.at[1], r_pair.at[:, pl.ds(3 * F + 2 * C, C)], y_branch.at[1], b1_pair)
    result, _ = scatter_end(2, False, out_last)
    o_block[...] = (mid_own[...] + result).astype(bf16)
    o_down[...] = grad_end(g_down, y_down, down_y, pl.ds(0, F))
    for k in range(2):
        total = grad_end(g_up, y_up, up_y if k == 0 else (), pl.ds(k * F, F))
        o_up[k] = total.T
    o_out[...] = grad_end(g_out, y_out, out_y, pl.ds(0, C))
    for copy in gg_copies:
        copy.wait_recv()
    total = gg_y[0].astype(f32) + gg_y[1].astype(f32) + gg_y[2].astype(f32) + gg_y[3].astype(f32)
    gg_f[core] = total
    gg_share = send(gg_f.at[core], gg_f.at[core], other)

    grad_n, q = scatter_end(3, True, last)
    v = tokens[...].astype(f32)
    s = scale1[...]
    gain = gains[0:1].astype(f32)
    o_tokens[...] = gmid_own[...] + s * gain * grad_n - v * s * s * q * (1.0 / D)
    small[0:1, :W] = jnp.sum(grad_n * v * s, axis=0, keepdims=True)
    small_pair = send(small, small_r, other)
    for k, copies in ((0, b0_y), (1, b1_y)):
        tp[pl.ds(0, C)] = grad_end(g_branch.at[k], y_branch.at[k], copies, pl.ds(0, C))
        o_branch[k] = tp[...].T[:, :C]
    small_pair.wait_recv()
    small_y[y] = small[...] + small_r[...]
    small_copies = [send(small_y.at[y], small_y.at[y], on_y(d)) for d in (2, 1, 3)]
    gg_share.wait_recv()
    for k in range(2):
        o_gates[k, 0] = gg_f[k, :, :C]
    for copy in small_copies:
        copy.wait_recv()
    total = small_y[0] + small_y[1] + small_y[2] + small_y[3]
    o_gains[...] = total[0:2, :W]
    o_conv[...] = total[2:6, :C]
    o_bias[...] = total[6:9, :C]
    o_decay[...] = total[9:10, :C]
    for copy in sent:
        copy.wait_send()


def on_device(
    tokens, doc_lengths, cotangent, norm_gains, w_branch, conv_weight, lru_bias, decay, gate_weights, w_out, w_up, w_down
):
    def shape(dims, kind=f32):
        return jax.ShapeDtypeStruct(dims, kind)

    def vmem(*dims, kind=f32):
        return pltpu.VMEM(dims, kind)

    def low(*dims):
        return pltpu.VMEM(dims, bf16)

    near, far = pl.BlockSpec(memory_space=pltpu.VMEM), pl.BlockSpec(memory_space=pl.ANY)
    rows = 3 * F + 3 * C
    scratch = (
        [low(2, D, C), low(2, 1, C, C), low(C, D), low(2, D, F), low(F, D)]
        + [low(2, 4, 4, H + Q, W)] + [low(2, 4, 4, H, W)] * 3 + [low(T, D)] * 4
        + [low(2, 4, 4 * H + Q, W)] * 4
        + [low(4, 2, 3, 4 * H + Q, W), low(4, 2, 4, H + Q, W), low(4, 2, 3, H + Q, W)]
        + [vmem(T + 8, C)] + [vmem(T, C)] * 13 + [vmem(T + 8, C), vmem(2 * H + T, C), vmem(2 * H + T, C), vmem(T, T)]
        + [vmem(8, W), vmem(T, F), vmem(T, W), vmem(T, W), vmem(T, W), vmem(T, W)]
        + [low(2, 4, F, 256), low(2, 4, 2 * F, 256), low(2, 4, C, 256), low(2, 2, 4, C, 256)]
        + [low(3, F, 256), low(3, 2 * F, 256), low(3, C, 256), low(2, 3, C, 256), low(4, rows, 256)]
        + [vmem(8, 256)] * 4 + [vmem(8, 256), vmem(3, 8, 256)] * 2
        + [low(2, C, 256), low(C, 256), low(4, C, 256), vmem(2, C, 256)]
        + [vmem(16, 256), vmem(16, 256), vmem(4, 16, 256)]
        + [pltpu.SemaphoreType.DMA((N_SEMS,)), pltpu.SemaphoreType.DMA((N_SEMS,)), pltpu.SemaphoreType.DMA((8,))]
    )
    outs = pl.pallas_call(
        kernel,
        out_shape=[
            shape((T, W), bf16), shape((T, W)), shape((2, W)), shape((2, 256, C)), shape((4, C)), shape((3, C)),
            shape((1, C)), shape((2, 1, C, C)), shape((C, 256)), shape((2, 256, F)), shape((F, 256)), shape((1, C)),
        ],
        in_specs=[near, pl.BlockSpec(memory_space=pltpu.SMEM)] + [near] * 5 + [far] * 5,
        out_specs=[near] * 12,
        scratch_shapes=scratch,
        compiler_params=pltpu.CompilerParams(
            collective_id=0, has_side_effects=True, vmem_limit_bytes=62 * 2**20
        ),
    )(
        tokens.reshape(T, W), doc_lengths, cotangent.reshape(T, W), norm_gains, conv_weight, lru_bias,
        decay.reshape(1, C), w_branch, gate_weights, w_out, w_up, w_down,
    )
    outs = list(outs)
    outs[0], outs[1] = outs[0].reshape(1, T, W), outs[1].reshape(1, T, W)
    outs[6], outs[11] = outs[6].reshape(C), outs[11].reshape(1, 1, C)
    return tuple(outs)


def solution(mesh):
    in_specs = (
        P("dp", "seq", "mp"), P("dp", None), P("dp", "seq", "mp"), P(None, "mp"), P(None, None, "mp"), P(None, "mp"),
        P(None, "mp"), P("mp"), P(None, "mp", None, None), P("mp", None), P(None, None, "mp"), P("mp", None),
    )
    out_specs = (
        P("dp", "seq", "mp"), P("dp", "seq", "mp"), P(None, "mp"), P(None, ("dp", "seq"), "mp"), P(None, "mp"),
        P(None, "mp"), P("mp"), P(None, "mp", None, None), P("mp", ("dp", "seq")), P(None, ("dp", "seq"), "mp"),
        P("mp", ("dp", "seq")), P("dp", "seq", "mp"),
    )
    return jax.shard_map(on_device, mesh=mesh, in_specs=in_specs, out_specs=out_specs, check_vma=False)
```

time: 1190 us -> 138 us (0.12)
  waiting for transfers between devices: 660 us -> 0 us
  local copies, waits for them, and re-layouts: 277 us -> 18.4 us
  Pallas kernels: 0 us -> 118 us
  other arithmetic: 107 us -> 0 us
  blocking collectives: 72.1 us -> 0 us
  matrix products: 37.6 us -> 0 us
  between operations: 15.9 us -> 0.68 us
    reduce_scatter x6 -> x0, waiting for transfers between devices: 316 us -> none  [the longest x2 148 us: reduce_out(): return lax.psum_scatter(partial_sums, 'mp', scatter_dimension=2, tiled=True)]
    psum x3 -> x0, waiting for transfers between devices: 204 us -> none  [the longest x2 179 us: norm_back(): grad_full = lax.psum(grad_part, 'mp')]
    slice x99 -> x0, local copies, waits for them, and re-layouts: 155 us -> none  [the longest x42 99.2 us: on_device(): through, local_state = lax.associative_scan(combine, (coef, drive), axis=1)]
    all_gather x4 -> x0, waiting for transfers between devices: 134 us -> none  [the longest x1 43.6 us: on_device(): lax.all_gather(middle_low, 'mp', axis=2, tiled=True).astype(jnp.float32)]
    pallas_call x0 -> x1, Pallas kernels: none -> 118 us  [on_device(): pl.pallas_call(kernel, out_shape=[shape((T, W), bf16), shape((T, W)), sha...]
    pad x56 -> x0, local copies, waits for them, and re-layouts: 108 us -> none  [the longest x28 83.2 us: on_device(): through, local_state = lax.associative_scan(combine, (coef, drive), axis=1)]
    add x50 -> x0, other arithmetic: 48.1 us -> none  [the longest x14 22 us: combine(): return (earlier[0] * later[0], later[0] * earlier[1] + later[1])]
    all_gather x4 -> x0, blocking collectives: 41.2 us -> none  [the longest x3 22.5 us: carried_in(): everything = jax.tree.map(lambda part: lax.all_gather(part, axis), array)]
  transfers between devices with their start and end apart: 15 -> 0, of which waited for: 14 -> 0; matrix products, arithmetic and copies ran while one was open for 5% -> 0% of each run, Pallas kernels for 0% -> 0%
where the time goes in v1:
time: 138 us; the launch traced here: 137 us
  Pallas kernels  118 us (86%)
  local copies, waits for them, and re-layouts  18.4 us (13%)
    pallas_call x1, Pallas kernels, on_device(): pl.pallas_call(kernel, out_shape=[shape((T, W), bf16), shape((T, W)), sha...  118 us
    unnamed x21, local copies, waits for them, and re-layouts  18.4 us

profile of v1, /device:TPU:1, one launch (start us, length us, event | category | flops | bytes accessed | tf_op | source)
XLA Modules:
  0.0 137.3 jit_solution(9841506610858081232)
XLA Ops:
  0.6 3.7 %copy.24.hbm_branch = bf16[2,2048,176]{2,1,0:T(8,128)(2,1)} copy(bf16[2,2048,176]{1,2,0:T(8,128)(2,1)} %param.16) | data formatting | bytes 2883584 | tf_op args[4]
  4.3 118.3 %shard_map.211 = (bf16[256,128]{1,0:T(8,128)(2,1)}, f32[256,128]{1,0:T(8,128)}, f32[2,128]{1,0:T(2,128)}, f32[2,256,176]{2,1,0:T(8,128)}, f32[4,176]{1,0:T(4,128...) custom-call(bf16[256,128]{1,0:T(8,128)(2,1)} %bitcast.8, ...), custom_call_target="tpu_custom_call" | custom-call | tf_op jit(solution)/shard_map/pallas_call | solution.py:578
  122.6 0.0 copy-start.2
  122.6 0.0 copy-start
  122.6 0.0 copy-start.1
  122.6 2.1 %copy.25 = f32[2,256,176]{1,2,0:T(8,128)} copy(f32[2,256,176]{2,1,0:T(8,128)} %get-tuple-element.39) | data formatting | bytes 720896
  124.7 0.0 copy-start.3
  124.7 1.5 %copy.37 = bf16[1,256,128]{2,1,0:T(8,128)(2,1)} copy(bf16[1,256,128]{2,1,0:T(8,128)(2,1)} %bitcast.10) | data formatting | bytes 131072
  126.1 1.6 %copy.38 = f32[1,256,128]{2,1,0:T(8,128)} copy(f32[1,256,128]{2,1,0:T(8,128)} %bitcast.7) | data formatting | bytes 262144
  127.7 1.2 copy.39
  128.9 1.3 copy.40
  130.2 1.3 copy.41
  131.5 1.2 copy.42
  132.7 1.7 %copy.43 = f32[2,1,176,176]{3,2,1,0:T(8,128)} copy(f32[2,1,176,176]{3,2,1,0:T(8,128)} %get-tuple-element.67) | data formatting | bytes 495616
  134.5 0.0 copy-done.2
  134.5 0.7 copy.44
  135.1 0.0 copy-done
  135.1 0.9 copy.45
  136.0 0.0 copy-done.1
  136.0 0.7 copy.46
  136.8 0.0 copy-done.3
  136.8 0.6 copy.47
Async XLA Ops:
  122.6 11.9 %copy-start.2 = (f32[176,256]{1,0:T(8,128)S(1)}, f32[176,256]{1,0:T(8,128)}, u32[]{:S(2)}) copy-start(f32[176,256]{1,0:T(8,128)} %get-tuple-element.68) | copy-start | bytes 540676
  122.6 12.6 %copy-start = (f32[2,256,384]{2,1,0:T(8,128)S(1)}, f32[2,256,384]{2,1,0:T(8,128)}, u32[]{:S(2)}) copy-start(f32[2,256,384]{2,1,0:T(8,128)} %get-tuple-element.69) | copy-start | bytes 2359300
  122.6 13.4 %copy-start.1 = (f32[384,256]{1,0:T(8,128)S(1)}, f32[384,256]{1,0:T(8,128)}, u32[]{:S(2)}) copy-start(f32[384,256]{1,0:T(8,128)} %get-tuple-element.70) | copy-start | bytes 1179652
  124.7 12.1 %copy-start.3 = (f32[1,176]{1,0:T(1,128)S(1)}, f32[1,176]{1,0:T(1,128)}, u32[]{:S(2)}) copy-start(f32[1,176]{1,0:T(1,128)} %get-tuple-element.35) | copy-start | bytes 2116

commit v2 on v1

v2 whole, which is shorter than its diff:
```python
import jax
import jax.numpy as jnp
from jax import lax
from jax.experimental import pallas as pl
from jax.experimental.pallas import tpu as pltpu
from jax.sharding import PartitionSpec as P

MESH = pl.DeviceIdType.MESH
f32, bf16 = jnp.float32, jnp.bfloat16

T, D, C, F, W = 256, 2048, 176, 384, 128
H = T // 2
EPS = 1e-06
N_SEMS, N_SENT = 104, 24
Q = 16
ALPHA, CUBIC = 0.7978845608028654, 0.044715
FAR_FIRST = (2, 1, 3)


def nn(a, b):
    return lax.dot_general(a, b, (((1,), (0,)), ((), ())), preferred_element_type=f32)


def nt(a, b):
    return lax.dot_general(a, b, (((1,), (1,)), ((), ())), preferred_element_type=f32)


def sigmoid(v):
    return 1.0 / (1.0 + jnp.exp(-v))


def gelu_both(v):
    square = v * v
    t = jnp.tanh(ALPHA * v * (1.0 + CUBIC * square))
    half = 0.5 * (1.0 + t)
    return v * half, half + 0.5 * v * (1.0 - t * t) * ALPHA * (1.0 + 3.0 * CUBIC * square)


def rider_tile(row):
    high = row.astype(bf16).astype(f32)
    index = lax.broadcasted_iota(jnp.int32, (Q, H), 0)
    return jnp.where(index == 0, high, jnp.where(index == 1, row - high, 0.0)).astype(bf16)


def kernel(
    lengths, gains, conv_w, bias, decay, hbm_tokens, hbm_cot, hbm_branch, hbm_gates, hbm_out, hbm_up, hbm_down,
    h_block, h_tokens, h_gains, h_branch, h_conv, h_bias, h_decay, h_gates, h_out, h_up, h_down, h_states,
    tokens, cot, w_branch, gates, w_out, w_up, w_down,
    o_block, o_tokens, o_gains, o_branch, o_conv, o_bias, o_decay, o_gates, o_out, o_up, o_down, o_states,
    tok_g, cot_g, mid_g, gm_g, first, second, cot_d, gm_d,
    part1, part2, part3, part4, rs_r1, rs_s2, rs_r2,
    ext, conv, aa, rr, ii, qq, coef, through, local, p0, p1, gel, dgel, state, prev, pad_a, pad_b, tp,
    ghid, mid_own, gmid_own, scale1, scale2,
    g_mlp, r_mlp, relay_mlp, y_mlp, g_rec, r_rec, relay_rec, y_rec,
    halo_s, halo_r, back_s, back_r, car_s, car_r, rev_s, rev_r,
    gg, gg_r, gg_y, gg_f, small, ruler,
    send_sems, recv_sems, copy_sems,
):
    me, seq, dp = lax.axis_index("mp"), lax.axis_index("seq"), lax.axis_index("dp")
    x, z = me // 4, me % 4
    core, y = seq % 2, (seq // 2) * 2 + dp

    def turn(value, by):
        return lax.rem(value + by + 4, 4)

    def on_x(d):
        return {"mp": turn(x, d) * 4 + z}

    def on_z(d):
        return {"mp": x * 4 + turn(z, d)}

    def on_y(d, same=True):
        there = turn(y, d)
        return {"dp": there % 2, "seq": (there // 2) * 2 + (core if same else 1 - core)}

    def on_seq(d):
        return {"seq": turn(seq, d)}

    other = on_y(0, False)

    groups, sources, stores = [], [], []

    def wait_bytes(sem, size):
        ref = ruler.at[pl.ds(0, size // (4 * W))]
        pltpu.make_async_copy(ref, ref, sem).wait()

    class Group:
        def __init__(self, kin=groups):
            self.i, self.size, self.done = len(kin), 0, False
            kin.append(self)

        def wait(self):
            if not self.done:
                self.done = True
                wait_bytes(recv_sems.at[self.i], self.size)

    def send(src, dst, where, group, source):
        size = src.dtype.itemsize
        for dim in src.shape:
            size *= dim
        group.size += size
        source.size += size
        pltpu.make_async_remote_copy(
            src_ref=src, dst_ref=dst, send_sem=send_sems.at[source.i], recv_sem=recv_sems.at[group.i],
            device_id=where, device_id_type=MESH,
        ).start()

    def send_one(src, dst, where):
        group = Group()
        send(src, dst, where, group, misc)
        return group

    misc = Group(sources)

    barrier = pltpu.get_barrier_semaphore()
    partners = [on_x(d) for d in (1, 2, 3)] + [on_z(d) for d in (1, 2, 3)] + [on_y(d) for d in (1, 2, 3)]
    partners += [on_y(d, False) for d in (0, 1, 2, 3)]
    for where in partners:
        pl.semaphore_signal(barrier, inc=1, device_id=where, device_id_type=MESH)

    loads = []

    def load(src, dst):
        copy = pltpu.make_async_copy(src, dst, copy_sems.at[len(loads)])
        copy.start()
        loads.append(copy)
        return copy

    def store(src, dst):
        copy = pltpu.make_async_copy(src, dst, copy_sems.at[16 + len(stores)])
        copy.start()
        stores.append(copy)

    load_tokens, load_cot = load(hbm_tokens, tokens), load(hbm_cot, cot)
    load_branch, load_gates, load_out = load(hbm_branch, w_branch), load(hbm_gates, gates), load(hbm_out, w_out)
    load_down, load_up = load(hbm_down, w_down), load(hbm_up, w_up)

    def finish():
        for group in groups:
            group.wait()
        for copy in stores:
            copy.wait()
        for source in sources:
            wait_bytes(send_sems.at[source.i], source.size)

    def axis_of(h, phase):
        return (on_x, on_z)[(h + phase) % 2]

    def place(h, first_hop, second_hop):
        return (turn(x, first_hop), turn(z, second_hop)) if h == 0 else (turn(x, second_hop), turn(z, first_hop))

    class Gather:
        def __init__(self, buf, rows):
            self.buf, self.rows = buf, rows
            self.arrivals, self.source = [], Group(sources)
            for d in (1, 3, 2):
                for h in range(2):
                    ref, group = self.view(h, x, z), Group()
                    send(ref, ref, axis_of(h, 0)(d), group, self.source)
                    self.arrivals.append((h, d, group))
            self.last = Group()
            for h in range(2):
                self.pass_on(h, 0)

        def view(self, h, cx, cz):
            return self.buf.at[h, cx, cz, pl.ds(0, self.rows[h])]

        def pass_on(self, h, d):
            ref = self.view(h, *place(h, -d, 0))
            for e in (1, 3, 2):
                send(ref, ref, axis_of(h, 1)(e), self.last, self.source)

        def forward(self):
            for h, d, group in self.arrivals:
                group.wait()
                self.pass_on(h, d)

        def end(self):
            self.last.wait()

    class Scatter:
        def __init__(self, n, part, rider):
            self.n, self.part, self.rider = n, part, rider
            self.source = Group(sources)
            self.hop1 = {(h, r): Group() for h in range(2) for r in range(4)}
            self.hop2 = [Group(), Group()]

        def rows(self, r):
            return pl.ds(0, H + Q if self.rider and r == 2 else H)

        def launch(self, g):
            n, part = self.n, self.part
            for d in FAR_FIRST:
                at = self.rows(g)
                src = part.at[0, turn(x, g), turn(z, d), at]
                send(src, rs_r1.at[n, 0, g, d - 1, at], on_z(d), self.hop1[0, g], self.source)
            if g:
                for r in FAR_FIRST + (0,):
                    at = self.rows(r)
                    src = part.at[1, turn(x, g), turn(z, r), at]
                    send(src, rs_r1.at[n, 1, r, g - 1, at], on_x(g), self.hop1[1, r], self.source)

        def produce(self, columns):
            for g in FAR_FIRST + (0,):
                there = turn(x, g)
                low = columns(pl.multiple_of(there * 512, 512)).astype(bf16)
                for c in range(4):
                    piece = low[:, c * W : (c + 1) * W]
                    self.part[0, there, c, pl.ds(0, H)] = piece[:H]
                    self.part[1, there, c, pl.ds(0, H)] = piece[H:]
                self.launch(g)

        def ride(self, products):
            for h in range(2):
                tile = rider_tile(jnp.sum(products[h * H : (h + 1) * H].T, axis=0, keepdims=True))
                if h == 0:
                    for c in range(4):
                        self.part[0, turn(x, 2), c, pl.ds(H, Q)] = tile
                else:
                    for c in range(4):
                        self.part[1, c, turn(z, 2), pl.ds(H, Q)] = tile

        def middle(self):
            n, part = self.n, self.part
            self.own, self.row = {}, {}
            for h, r in ((0, 2), (0, 1), (1, 2), (0, 3), (1, 1), (1, 3), (0, 0), (1, 0)):
                self.hop1[h, r].wait()
                spot = (turn(x, r), z) if h == 0 else (x, turn(z, r))
                total = part[h, *spot, pl.ds(0, H)].astype(f32)
                for d in range(3):
                    total += rs_r1[n, h, r, d, pl.ds(0, H)].astype(f32)
                if self.rider and r == 2:
                    rider = part[h, *spot, pl.ds(H, Q)].astype(f32)
                    for d in range(3):
                        rider += rs_r1[n, h, r, d, pl.ds(H, Q)].astype(f32)
                    self.row[h] = jnp.sum(rider, axis=0, keepdims=True)
                    tile = rider_tile(self.row[h])
                    for k in range(3):
                        rs_s2[n, h, k, pl.ds(H, Q)] = tile
                if r:
                    rs_s2[n, h, r - 1, pl.ds(0, H)] = total.astype(bf16)
                    at = pl.ds(0, H + Q if self.rider else H)
                    where = axis_of(h, 0)(r)
                    send(rs_s2.at[n, h, r - 1, at], rs_r2.at[n, h, r - 1, at], where, self.hop2[h], self.source)
                else:
                    self.own[h] = total

        def end(self):
            n, out, column = self.n, [], []
            for h in range(2):
                total, row = self.own[h], self.row.get(h)
                self.hop2[h].wait()
                for r in (1, 3, 2):
                    total += rs_r2[n, h, r - 1, pl.ds(0, H)].astype(f32)
                    if self.rider:
                        row += jnp.sum(rs_r2[n, h, r - 1, pl.ds(H, Q)].astype(f32), axis=0, keepdims=True)
                out.append(total)
                if self.rider:
                    column.append(jnp.broadcast_to(row, (H, H)).T)
            return jnp.concatenate(out, 0), (jnp.concatenate(column, 0) if self.rider else None)

    def chunk(buf, c):
        return jnp.concatenate([buf[0, c // 4, c % 4, pl.ds(0, H)], buf[1, c // 4, c % 4, pl.ds(0, H)]], 0)

    def gain_row(k, c):
        return tok_g[0, c // 4, c % 4, pl.ds(H, Q)].astype(f32)[k : k + 1]

    def norm(buf, k, scale_ref, dst):
        total = jnp.zeros((T, W), f32)
        for c in range(16):
            v = chunk(buf, c).astype(f32)
            total += v * v
        scale = lax.rsqrt(jnp.sum(total, axis=1, keepdims=True) * (1.0 / D) + EPS)
        scale_ref[...] = jnp.broadcast_to(scale, (T, W))
        for c in range(16):
            v = chunk(buf, c).astype(f32)
            dst[:, c * W : (c + 1) * W] = (v * scale_ref[...] * gain_row(k, c)).astype(bf16)

    def dense(buf, dst):
        for c in range(16):
            dst[:, c * W : (c + 1) * W] = chunk(buf, c)

    class WeightGrad:
        def __init__(self, g, r, relay, into, rows):
            self.g, self.r, self.relay, self.into, self.rows = g, r, relay, into, rows
            cut = rows // 32 * 16 + (16 if rows % 32 else 0)
            self.a, self.b = pl.ds(0, cut), pl.ds(cut, rows - cut)

        def compute(self, left, right):
            for there in range(4):
                for core_there in range(2):
                    j = (there % 2) * 4 + (there // 2) * 2 + core_there
                    self.g[core_there, there] = nn(left, right[:, j * 256 : (j + 1) * 256]).astype(bf16)

        def start(self):
            self.source = Group(sources)
            self.pair = Group()
            send(self.g.at[1 - core], self.r, other, self.pair, self.source)

        def add(self, there, at, other_part):
            g = self.g
            g[core, there, at] = (g[core, there, at].astype(f32) + other_part.astype(f32)).astype(bf16)

        def middle(self):
            self.pair.wait()
            g, a, b = self.g, self.a, self.b
            self.relayed, self.last = Group(), Group()
            far = turn(y, 2)
            self.add(far, pl.ds(0, self.rows), self.r[far])
            send(g.at[core, far, a], self.relay.at[a], on_y(1), self.relayed, self.source)
            send(g.at[core, far, b], self.relay.at[b], on_y(-1), self.relayed, self.source)
            for k, at in ((1, b), (-1, a)):
                there = turn(y, k)
                self.add(there, pl.ds(0, self.rows), self.r[there])
                send(g.at[core, there, at], self.into.at[(1 - k) // 2, at], on_y(k), self.last, self.source)
            self.add(y, pl.ds(0, self.rows), self.r[y])

        def pass_on(self):
            self.relayed.wait()
            for k, at in ((1, self.a), (-1, self.b)):
                there = turn(y, k)
                self.add(there, at, self.relay[at])
                send(self.g.at[core, there, at], self.into.at[(1 - k) // 2, at], on_y(k), self.last, self.source)

        def end(self):
            self.last.wait()
            return self.g[core, y].astype(f32) + self.into[0].astype(f32) + self.into[1].astype(f32)

    def transposed(value):
        tp[:, :C] = value
        return tp[...].T[:C]

    def weight_grad(i, rows):
        refs = (g_mlp, r_mlp, relay_mlp, y_mlp) if rows == F else (g_rec, r_rec, relay_rec, y_rec)
        return WeightGrad(*[ref.at[i] for ref in refs], rows)

    down, up = weight_grad(0, F), [weight_grad(1, F), weight_grad(2, F)]
    out, branches = weight_grad(0, C), [weight_grad(1, C), weight_grad(2, C)]

    gain_tile = jnp.concatenate([gains[...].astype(f32), jnp.zeros((Q - 2, W), f32)], 0).astype(bf16)
    tok_g[0, x, z, pl.ds(H, Q)] = gain_tile
    load_tokens.wait()
    load_cot.wait()
    for h in range(2):
        tok_g[h, x, z, pl.ds(0, H)] = tokens[pl.ds(h * H, H)]
        cot_g[h, x, z] = cot[pl.ds(h * H, H)]
    tp[...] = jnp.zeros_like(tp)
    pl.semaphore_wait(barrier, len(partners))
    tok_gather = Gather(tok_g, (H + Q, H))
    tok_gather.forward()
    cot_gather = Gather(cot_g, (H, H))

    place_here = lax.broadcasted_iota(jnp.int32, (T, 1), 0) + seq * T
    start, begins = 0, [0]
    for j in range(3):
        start = start + lengths[0, j]
        begins.append(start)

    def begin_at(p):
        hit = p == begins[0]
        for b in begins[1:]:
            hit = jnp.logical_or(hit, p == b)
        return hit

    not_reset = jnp.where(begin_at(place_here), 0.0, 1.0)
    masks = [not_reset]
    for k in (1, 2):
        masks.append(masks[-1] * jnp.where(begin_at(place_here - k), 0.0, 1.0))

    tok_gather.end()
    norm(tok_g, 0, scale1, first)
    load_branch.wait()
    load_gates.wait()

    value = nt(first[...], w_branch[1])
    p1[...] = value
    inner = value.astype(bf16).astype(f32)
    ext[pl.ds(8, T)] = inner
    halo_s[:, :C] = inner[T - 8 :]
    halo = send_one(halo_s, halo_r, on_seq(1))
    value = nt(first[...], w_branch[0])
    p0[...] = value
    act, slope = gelu_both(value)
    gel[...] = act
    dgel[...] = slope
    cot_gather.forward()
    halo.wait()
    ext[pl.ds(0, 8)] = halo_r[:, :C]
    total = bias[0:1] + conv_w[0:1] * ext[pl.ds(8, T)]
    for k in (1, 2, 3):
        total = total + conv_w[k : k + 1] * (masks[k - 1] * ext[pl.ds(8 - k, T)])
    conv[...] = total
    conv_low = total.astype(bf16)
    rate = jax.nn.softplus(decay[...])
    r_gate = sigmoid(nn(conv_low, gates[0, 0]) + bias[1:2])
    rr[...] = r_gate
    a = jnp.exp(-8.0 * r_gate * rate)
    aa[...] = a
    coef[...] = a * not_reset
    i_gate = sigmoid(nn(conv_low, gates[1, 0]) + bias[2:3])
    ii[...] = i_gate
    root = jnp.sqrt(1.0 - a * a + 0.001)
    qq[...] = root

    def scan(A, B, reverse):
        step = 1
        while step < T:
            for ref, v, fill in ((pad_a, A, 1.0), (pad_b, B, 0.0)):
                ref[pl.ds(H, T)] = v
                ref[pl.ds(H + T if reverse else 0, H)] = jnp.full((H, C), fill, f32)
            at = pl.ds(H + step if reverse else H - step, T)
            B = B + A * pad_b[at]
            A = A * pad_a[at]
            step *= 2
        return A, B

    A, B = scan(coef[...], root * i_gate * conv[...], False)
    through[...] = A
    local[...] = B
    car_s[0:1, :C] = A[T - 1 :]
    car_s[1:2, :C] = B[T - 1 :]
    carries = Group()
    for d in (2, 1, 3):
        send(car_s, car_r.at[d - 1], on_seq(d), carries, misc)
    cot_gather.end()
    dense(cot_g, cot_d)
    load_out.wait()
    load_down.wait()
    load_up.wait()
    ghid[...] = nt(cot_d[...], w_down[...])
    carries.wait()

    def fold(got, reverse):
        carried = jnp.zeros((1, C), f32)
        for d in (3, 2, 1):
            here = (seq + d < 4) if reverse else (seq - d >= 0)
            slot = 4 - d if reverse else d
            new = got[slot - 1, 0:1, :C] * carried + got[slot - 1, 1:2, :C]
            carried = jnp.where(here, new, carried)
        return carried

    carried = fold(car_r, False)
    value = local[...] + through[...] * carried
    state[...] = value
    prev[pl.ds(8, T)] = value
    prev[7:8] = carried
    mixed = gel[...] * value
    mixed_low = mixed.astype(bf16)
    scatter = Scatter(0, part1, False)
    scatter.produce(lambda at: nn(mixed_low, w_out[:, pl.ds(at, 512)]))
    o_states[...] = value[T - 1 :]
    store(o_states, h_states)
    mixed_t = transposed(mixed).astype(bf16)
    scatter.middle()
    branch, _ = scatter.end()
    middle = tokens[...].astype(f32) + branch
    mid_own[...] = middle
    middle_low = middle.astype(bf16)
    for h in range(2):
        mid_g[h, x, z] = middle_low[h * H : (h + 1) * H]
    gather = Gather(mid_g, (H, H))
    gather.forward()
    gather.end()
    norm(mid_g, 1, scale2, second)

    pair0 = nn(second[...], w_up[0])
    pair1 = nn(second[...], w_up[1])
    act, slope = gelu_both(pair0)
    hidden = act * pair1
    gh = ghid[...]
    gp0 = slope * pair1 * gh
    gp1 = act * gh
    products = gp0 * pair0 + gp1 * pair1
    products = products[:, :W] + products[:, W : 2 * W] + products[:, 2 * W :]
    gp0_low, gp1_low = gp0.astype(bf16), gp1.astype(bf16)
    scatter = Scatter(1, part2, True)
    scatter.ride(products)
    scatter.produce(lambda at: nt(gp0_low, w_up[0, pl.ds(at, 512)]) + nt(gp1_low, w_up[1, pl.ds(at, 512)]))
    down.compute(hidden.T.astype(bf16), cot_d)
    down.start()
    up[0].compute(gp0.T.astype(bf16), second)
    up[0].start()
    down.middle()
    scatter.middle()
    up[1].compute(gp1.T.astype(bf16), second)
    up[1].start()
    up[0].middle()

    grad_n, q = scatter.end()
    v = mid_own[...].astype(bf16).astype(f32)
    s = scale2[...]
    gain = gains[1:2].astype(f32)
    grad_middle_own = cot[...].astype(f32) + s * gain * grad_n - v * s * s * q * (1.0 / D)
    gmid_own[...] = grad_middle_own
    low = grad_middle_own.astype(bf16)
    for h in range(2):
        gm_g[h, x, z] = low[h * H : (h + 1) * H]
    gather = Gather(gm_g, (H, H))
    mine = small.at[dp * 4 + seq]
    mine[...] = jnp.zeros((16, 256), f32)
    mine[1:2, :W] = jnp.sum(grad_n * v * s, axis=0, keepdims=True)
    gather.forward()
    down.pass_on()
    up[1].middle()
    up[0].pass_on()
    hidden_low = hidden.astype(bf16)
    gather.end()
    dense(gm_g, gm_d)

    grad_mixed = nt(gm_d[...], w_out[...])
    grad_y = dgel[...] * state[...] * grad_mixed
    grad_state = gel[...] * grad_mixed
    pad_a[pl.ds(0, T)] = coef[...]
    pad_a[pl.ds(T, 8)] = jnp.ones((8, C), f32)
    A, B = scan(pad_a[pl.ds(1, T)], grad_state, True)
    rev_s[0:1, :C] = through[T - 1 :]
    rev_s[1:2, :C] = coef[0:1] * B[0:1]
    carries = Group()
    for d in (2, 1, 3):
        send(rev_s, rev_r.at[d - 1], on_seq(d), carries, misc)
    scatter_out = Scatter(2, part3, False)
    scatter_out.produce(lambda at: nn(hidden_low, w_down[:, pl.ds(at, 512)]))
    out.compute(mixed_t, gm_d)
    out.start()
    carries.wait()
    total = B + A * fold(rev_r, True)
    a, r_gate, i_gate, root, cv = aa[...], rr[...], ii[...], qq[...], conv[...]
    t_i = total * i_gate
    d_log = total * prev[pl.ds(7, T)] * coef[...] - t_i * cv * (a * a / root)
    d_gate = d_log * r_gate
    mine[9:10, :C] = -8.0 * sigmoid(decay[...]) * jnp.sum(d_gate, axis=0, keepdims=True)
    gpre0 = -8.0 * rate * d_gate * (1.0 - r_gate)
    direct = t_i * root
    gpre1 = direct * cv * (1.0 - i_gate)
    low0, low1 = gpre0.astype(bf16), gpre1.astype(bf16)
    mine[7:8, :C] = jnp.sum(low0.astype(f32), axis=0, keepdims=True)
    mine[8:9, :C] = jnp.sum(low1.astype(f32), axis=0, keepdims=True)
    grad_conv = direct + nt(low0, gates[0, 0]) + nt(low1, gates[1, 0])
    mine[6:7, :C] = jnp.sum(grad_conv, axis=0, keepdims=True)
    edge = jnp.zeros((8, C), f32)
    grad_inner = jnp.zeros((T, C), f32)
    for k in range(4):
        weighted = grad_conv if k == 0 else masks[k - 1] * grad_conv
        mine[2 + k : 3 + k, :C] = jnp.sum(weighted * ext[pl.ds(8 - k, T)], axis=0, keepdims=True)
        if k == 0:
            pad_a[pl.ds(0, 8)] = jnp.zeros((8, C), f32)
            pad_a[pl.ds(8 + T, 8)] = jnp.zeros((8, C), f32)
        pad_a[pl.ds(8, T)] = conv_w[k : k + 1] * weighted
        edge += pad_a[pl.ds(k, 8)]
        grad_inner += pad_a[pl.ds(8 + k, T)]
    back_s[:, :C] = edge
    back = send_one(back_s, back_r, on_seq(-1))
    cv_t = transposed(cv).astype(bf16)
    gg[0, :, :C] = nn(cv_t, low0).astype(bf16)
    gg[1, :, :C] = nn(cv_t, low1).astype(bf16)
    gg_pair = send_one(gg.at[1 - core], gg_r, other)
    up[1].pass_on()
    scatter_out.middle()
    out.middle()
    branches[0].compute(transposed(grad_y).astype(bf16), first)
    branches[0].start()
    back.wait()
    ext[pl.ds(0, T)] = grad_inner
    ext[pl.ds(T - 8, 8)] = grad_inner[T - 8 :] + back_r[:, :C]
    grad_inner = ext[pl.ds(0, T)]
    gpr0, gpr1 = grad_y.astype(bf16), grad_inner.astype(bf16)
    tp[:, :C] = grad_y * p0[...] + grad_inner * p1[...]
    scatter = Scatter(3, part4, True)
    scatter.ride(tp[:, :W] + tp[:, W:])
    scatter.produce(lambda at: nn(gpr0, w_branch[0, :, pl.ds(at, 512)]) + nn(gpr1, w_branch[1, :, pl.ds(at, 512)]))
    branches[1].compute(transposed(grad_inner).astype(bf16), first)
    branches[1].start()
    branches[0].middle()
    gg_pair.wait()
    gg_y[y] = (gg[core].astype(f32) + gg_r[...].astype(f32)).astype(bf16)
    gg_all = Group()
    for d in FAR_FIRST:
        send(gg_y.at[y], gg_y.at[y], on_y(d), gg_all, misc)
    out.pass_on()
    scatter.middle()
    branches[1].middle()
    branches[0].pass_on()
    result, _ = scatter_out.end()
    o_block[...] = (mid_own[...] + result).astype(bf16)
    store(o_block, h_block)
    o_down[...] = down.end()
    store(o_down, h_down)
    for k in range(2):
        o_up[k] = up[k].end().T
    store(o_up, h_up)
    branches[1].pass_on()
    o_out[...] = out.end()
    store(o_out, h_out)
    gg_all.wait()
    gg_f[core] = gg_y[0].astype(f32) + gg_y[1].astype(f32) + gg_y[2].astype(f32) + gg_y[3].astype(f32)
    gg_share = send_one(gg_f.at[core], gg_f.at[core], other)

    grad_n, q = scatter.end()
    v = tokens[...].astype(f32)
    s = scale1[...]
    gain = gains[0:1].astype(f32)
    mine[0:1, :W] = jnp.sum(grad_n * v * s, axis=0, keepdims=True)
    smalls = Group()
    for d, same in ((2, False), (2, True), (1, False), (1, True), (3, False), (3, True), (0, False)):
        send(mine, mine, on_y(d, same), smalls, misc)
    o_tokens[...] = gmid_own[...] + s * gain * grad_n - v * s * s * q * (1.0 / D)
    store(o_tokens, h_tokens)
    for k in range(2):
        o_branch[k] = branches[k].end()
    store(o_branch, h_branch)
    gg_share.wait()
    for k in range(2):
        o_gates[k, 0] = gg_f[k, :, :C]
    store(o_gates, h_gates)
    smalls.wait()
    total = small[0]
    for j in range(1, 8):
        total += small[j]
    o_gains[...] = total[0:2, :W]
    o_conv[...] = total[2:6, :C]
    o_bias[...] = total[6:9, :C]
    o_decay[...] = total[9:10, :C]
    for src, dst in ((o_gains, h_gains), (o_conv, h_conv), (o_bias, h_bias), (o_decay, h_decay)):
        store(src, dst)
    finish()


def hand_over(*refs):
    n = 12
    ins, outs, held, (in_sems, out_sems) = refs[:n], refs[n : 2 * n], refs[2 * n : 3 * n], refs[3 * n :]
    copies = [pltpu.make_async_copy(ins[i], held[i], in_sems.at[i]) for i in range(n)]
    for copy in copies:
        copy.start()
    stores = []
    for i in range(n):
        copies[i].wait()
        stores.append(pltpu.make_async_copy(held[i], outs[i], out_sems.at[i]))
        stores[i].start()
    for copy in stores:
        copy.wait()


def on_device(
    tokens, doc_lengths, cotangent, norm_gains, w_branch, conv_weight, lru_bias, decay, gate_weights, w_out, w_up, w_down
):
    def shape(dims, kind=f32):
        return jax.ShapeDtypeStruct(dims, kind)

    def vmem(*dims):
        return pltpu.VMEM(dims, f32)

    def low(*dims):
        return pltpu.VMEM(dims, bf16)

    near, far = pl.BlockSpec(memory_space=pltpu.VMEM), pl.BlockSpec(memory_space=pl.ANY)
    outs = [
        shape((T, W), bf16), shape((T, W)), shape((2, W)), shape((2, C, 256)), shape((4, C)), shape((3, C)),
        shape((1, C)), shape((2, 1, C, C)), shape((C, 256)), shape((2, 256, F)), shape((F, 256)), shape((1, C)),
    ]
    scratch = (
        [low(T, W), low(T, W), low(2, C, D), low(2, 1, C, C), low(C, D), low(2, D, F), low(F, D)]
        + [pltpu.VMEM(o.shape, o.dtype) for o in outs]
        + [low(2, 4, 4, H + Q, W)] + [low(2, 4, 4, H, W)] * 3 + [low(T, D)] * 4
        + [low(2, 4, 4, H + Q, W)] * 4
        + [low(4, 2, 4, 3, H + Q, W), low(4, 2, 3, H + Q, W), low(4, 2, 3, H + Q, W)]
        + [vmem(T + 8, C)] + [vmem(T, C)] * 13 + [vmem(T + 8, C), vmem(2 * H + T, C), vmem(2 * H + T, C), vmem(T, T)]
        + [vmem(T, F), vmem(T, W), vmem(T, W), vmem(T, W), vmem(T, W)]
        + [low(3, 2, 4, F, 256), low(3, 4, F, 256), low(3, F, 256), low(3, 2, F, 256)]
        + [low(3, 2, 4, C, 256), low(3, 4, C, 256), low(3, C, 256), low(3, 2, C, 256)]
        + [vmem(8, 256)] * 4 + [vmem(8, 256), vmem(3, 8, 256)] * 2
        + [low(2, C, 256), low(C, 256), low(4, C, 256), vmem(2, C, 256)]
        + [vmem(8, 16, 256), vmem(6144, W)]
        + [pltpu.SemaphoreType.DMA((N_SENT,)), pltpu.SemaphoreType.DMA((N_SEMS,)), pltpu.SemaphoreType.DMA((32,))]
    )
    made = pl.pallas_call(
        kernel,
        out_shape=outs,
        in_specs=[pl.BlockSpec(memory_space=pltpu.SMEM)] + [near] * 4 + [far] * 7,
        out_specs=[far] * 12,
        scratch_shapes=scratch,
        compiler_params=pltpu.CompilerParams(
            collective_id=0, has_side_effects=True, vmem_limit_bytes=62 * 2**20
        ),
    )(
        doc_lengths, norm_gains, conv_weight, lru_bias, decay.reshape(1, C), tokens.reshape(T, W),
        cotangent.reshape(T, W), jnp.swapaxes(w_branch, 1, 2), gate_weights, w_out, w_up, w_down,
    )
    made = list(pl.pallas_call(
        hand_over,
        out_shape=outs,
        in_specs=[far] * 12,
        out_specs=[far] * 12,
        scratch_shapes=[pltpu.VMEM(o.shape, o.dtype) for o in outs] + [pltpu.SemaphoreType.DMA((12,))] * 2,
        compiler_params=pltpu.CompilerParams(vmem_limit_bytes=62 * 2**20),
    )(*made))
    made[0], made[1] = made[0].reshape(1, T, W), made[1].reshape(1, T, W)
    made[3] = jnp.swapaxes(made[3], 1, 2)
    made[6], made[11] = made[6].reshape(C), made[11].reshape(1, 1, C)
    return tuple(made)


def solution(mesh):
    in_specs = (
        P("dp", "seq", "mp"), P("dp", None), P("dp", "seq", "mp"), P(None, "mp"), P(None, None, "mp"), P(None, "mp"),
        P(None, "mp"), P("mp"), P(None, "mp", None, None), P("mp", None), P(None, None, "mp"), P("mp", None),
    )
    out_specs = (
        P("dp", "seq", "mp"), P("dp", "seq", "mp"), P(None, "mp"), P(None, ("dp", "seq"), "mp"), P(None, "mp"),
        P(None, "mp"), P("mp"), P(None, "mp", None, None), P("mp", ("dp", "seq")), P(None, ("dp", "seq"), "mp"),
        P("mp", ("dp", "seq")), P("dp", "seq", "mp"),
    )
    return jax.shard_map(on_device, mesh=mesh, in_specs=in_specs, out_specs=out_specs, check_vma=False)
```

time: 138 us -> 103 us (0.75)
  local copies, waits for them, and re-layouts: 18.4 us -> 0 us
  Pallas kernels: 118 us -> 102 us
    unnamed x21 -> x0, local copies, waits for them, and re-layouts: 18.4 us -> none
    pallas_call x1 -> x2, Pallas kernels: 118 us -> 102 us  [the longest x1 99.5 us: on_device(): pl.pallas_call(kernel, out_shape=outs, in_specs=[pl.BlockSpec(memory_spac...]
where the time goes in v2:
time: 103 us
  Pallas kernels  102 us (99%)
    pallas_call x1, Pallas kernels, on_device(): pl.pallas_call(kernel, out_shape=outs, in_specs=[pl.BlockSpec(memory_spac...  99.5 us
    pallas_call x1, Pallas kernels, on_device(): pl.pallas_call(hand_over, out_shape=outs, in_specs=[far] * 12, out_specs=...  2.76 us

profile of v2, /device:TPU:1, one launch (start us, length us, event | category | flops | bytes accessed | tf_op | source)
XLA Modules:
  0.0 103.1 jit_solution(10580057945535507443)
XLA Ops:
  0.6 99.5 %shard_map.211 = (bf16[256,128]{1,0:T(8,128)(2,1)}, f32[256,128]{1,0:T(8,128)}, f32[2,128]{1,0:T(2,128)}, f32[2,176,256]{2,1,0:T(8,128)}, f32[4,176]{1,0:T(4,128...) custom-call(s32[1,4]{1,0:T(1,128)} %lengths.1, ...), custom_call_target="tpu_custom_call" | custom-call | tf_op jit(solution)/shard_map/pallas_call | solution.py:675
  100.2 2.8 %shard_map.212 = (bf16[256,128]{1,0:T(8,128)(2,1)}, f32[256,128]{1,0:T(8,128)}, f32[2,128]{1,0:T(2,128)}, f32[2,176,256]{2,1,0:T(8,128)}, f32[4,176]{1,0:T(4,128...) custom-call(bf16[256,128]{1,0:T(8,128)(2,1)} %get-tuple-element.36.r, ...), custom_call_target="tpu_custom_call" | custom-call | tf_op jit(solution)/shard_map/pallas_call | solution.py:688

commit v3 on v2

v3 whole, which is shorter than its diff:
```python
import jax
import jax.numpy as jnp
from jax import lax
from jax.experimental import pallas as pl
from jax.experimental.pallas import tpu as pltpu
from jax.sharding import PartitionSpec as P

MESH = pl.DeviceIdType.MESH
f32, bf16 = jnp.float32, jnp.bfloat16

T, D, C, F, W = 256, 2048, 176, 384, 128
H = T // 2
EPS = 1e-06
N_SEMS, N_SENT = 112, 28
CP = 256
LATE = 16
Q = 16
ALPHA, CUBIC = 0.7978845608028654, 0.044715
FAR_FIRST = (2, 1, 3)


def nn(a, b):
    return lax.dot_general(a, b, (((1,), (0,)), ((), ())), preferred_element_type=f32)


def nt(a, b):
    return lax.dot_general(a, b, (((1,), (1,)), ((), ())), preferred_element_type=f32)


def sigmoid(v):
    return 1.0 / (1.0 + jnp.exp(-v))


def gelu_both(v):
    square = v * v
    t = jnp.tanh(ALPHA * v * (1.0 + CUBIC * square))
    half = 0.5 * (1.0 + t)
    return v * half, half + 0.5 * v * (1.0 - t * t) * ALPHA * (1.0 + 3.0 * CUBIC * square)


def rider_tile(row):
    high = row.astype(bf16).astype(f32)
    index = lax.broadcasted_iota(jnp.int32, (Q, H), 0)
    return jnp.where(index == 0, high, jnp.where(index == 1, row - high, 0.0)).astype(bf16)


def kernel(
    lengths, gains, conv_w, bias, decay, hbm_tokens, hbm_cot, hbm_branch, hbm_gates, hbm_out, hbm_up, hbm_down,
    o_block, o_tokens, o_gains, o_branch, o_conv, o_bias, o_decay, o_gates, o_out, o_up, o_down, o_states,
    tokens, cot, w_branch, gates, w_out, w_up, w_down,
    tok_g, cot_g, mid_g, gm_g, first, second, cot_d, gm_d,
    part1, part2, part3, part4, rs_r1, rs_s2, rs_r2,
    ext, conv, aa, rr, ii, qq, coef, through, local, p0, p1, gel, dgel, state, prev, pad_a, pad_b, tp,
    ghid, mid_own, gmid_own, scale1, scale2,
    blocks, left_mlp, g_mlp, relay_mlp, y_mlp, left_rec, g_rec, relay_rec, y_rec, lhs,
    halo_s, halo_r, back_s, back_r, car_s, car_r, rev_s, rev_r,
    gg, gg_r, gg_y, gg_f, small, gain_one, ruler,
    send_sems, recv_sems, copy_sems,
):
    me, seq, dp = lax.axis_index("mp"), lax.axis_index("seq"), lax.axis_index("dp")
    x, z = me // 4, me % 4
    core, y = seq % 2, (seq // 2) * 2 + dp

    def turn(value, by):
        return lax.rem(value + by + 4, 4)

    def on_x(d):
        return {"mp": turn(x, d) * 4 + z}

    def on_z(d):
        return {"mp": x * 4 + turn(z, d)}

    def on_y(d, same=True):
        there = turn(y, d)
        return {"dp": there % 2, "seq": (there // 2) * 2 + (core if same else 1 - core)}

    def on_seq(d):
        return {"seq": turn(seq, d)}

    other = on_y(0, False)

    groups, sources = [], []

    def wait_bytes(sem, size):
        ref = ruler.at[pl.ds(0, size // (4 * W))]
        pltpu.make_async_copy(ref, ref, sem).wait()

    class Group:
        def __init__(self, kin=groups):
            self.i, self.size, self.done = len(kin), 0, False
            kin.append(self)

        def wait(self):
            if not self.done:
                self.done = True
                wait_bytes(recv_sems.at[self.i], self.size)

    def send(src, dst, where, group, source):
        size = src.dtype.itemsize
        for dim in src.shape:
            size *= dim
        group.size += size
        source.size += size
        pltpu.make_async_remote_copy(
            src_ref=src, dst_ref=dst, send_sem=send_sems.at[source.i], recv_sem=recv_sems.at[group.i],
            device_id=where, device_id_type=MESH,
        ).start()

    def send_one(src, dst, where):
        group = Group()
        send(src, dst, where, group, misc)
        return group

    misc = Group(sources)

    barrier = pltpu.get_barrier_semaphore()
    partners = [on_x(d) for d in (1, 2, 3)] + [on_z(d) for d in (1, 2, 3)] + [on_y(d) for d in (1, 2, 3)]
    partners += [on_y(d, False) for d in (0, 1, 2, 3)]
    for where in partners:
        pl.semaphore_signal(barrier, inc=1, device_id=where, device_id_type=MESH)

    loads = []

    def load(src, dst):
        copy = pltpu.make_async_copy(src, dst, copy_sems.at[len(loads)])
        copy.start()
        loads.append(copy)
        return copy

    load_tokens, load_cot = load(hbm_tokens, tokens), load(hbm_cot, cot)
    load_branch = [load(hbm_branch.at[k], w_branch.at[pl.ds(k * CP, C)]) for k in range(2)]
    load_gates, load_out = load(hbm_gates, gates), load(hbm_out, w_out.at[pl.ds(0, C)])
    load_down = load(hbm_down, w_down)
    load_up = [load(hbm_up.at[k], w_up.at[:, pl.ds(k * F, F)]) for k in range(2)]
    for rows in (w_branch.at[pl.ds(C, CP - C)], w_branch.at[pl.ds(CP + C, CP - C)], w_out.at[pl.ds(C, CP - C)], lhs):
        rows[...] = jnp.zeros(rows.shape, bf16)

    def finish():
        for group in groups:
            group.wait()
        for source in sources:
            wait_bytes(send_sems.at[source.i], source.size)

    def axis_of(h, phase):
        return (on_x, on_z)[(h + phase) % 2]

    def place(h, first_hop, second_hop):
        return (turn(x, first_hop), turn(z, second_hop)) if h == 0 else (turn(x, second_hop), turn(z, first_hop))

    class Gather:
        def __init__(self, buf, rows):
            self.buf, self.rows = buf, rows
            self.arrivals, self.source = [], Group(sources)
            for d in (1, 3, 2):
                for h in range(2):
                    ref, group = self.view(h, x, z), Group()
                    send(ref, ref, axis_of(h, 0)(d), group, self.source)
                    self.arrivals.append((h, d, group))
            self.last = Group()
            for h in range(2):
                self.pass_on(h, 0)

        def view(self, h, cx, cz):
            return self.buf.at[h, cx, cz, pl.ds(0, self.rows[h])]

        def pass_on(self, h, d):
            ref = self.view(h, *place(h, -d, 0))
            for e in (1, 3, 2):
                send(ref, ref, axis_of(h, 1)(e), self.last, self.source)

        def forward(self):
            for h, d, group in self.arrivals:
                group.wait()
                self.pass_on(h, d)

        def end(self):
            self.last.wait()

    class Scatter:
        def __init__(self, n, part, rider=False, late=False):
            self.n, self.part, self.rider, self.late = n, part, rider, late
            self.source = Group(sources)
            self.hop1 = {(h, r): Group() for h in range(2) for r in range(4)}
            self.hop2 = {h: Group() for h in range(2)}
            if late:
                self.hop1.update({(2, r): Group() for r in range(4)})
                self.hop2[2] = Group()
            self.own, self.row = {}, {}

        def rows(self, h, rider):
            first, size = ((0, H), (0, H - LATE if self.late else H), (H - LATE, LATE))[h]
            return pl.ds(first, size + (Q if rider and self.rides(h) else 0))

        def rides(self, h):
            return self.rider and h in ((0, 2) if self.late else (0, 1))

        def launch(self, g, halves):
            n, part = self.n, self.part
            for h in halves:
                if h == 0:
                    for d in FAR_FIRST:
                        at = self.rows(h, g == 2)
                        src = part.at[0, turn(x, g), turn(z, d), at]
                        send(src, rs_r1.at[n, 0, g, d - 1, at], on_z(d), self.hop1[0, g], self.source)
                elif g:
                    for r in FAR_FIRST + (0,):
                        at = self.rows(h, r == 2)
                        src = part.at[1, turn(x, g), turn(z, r), at]
                        send(src, rs_r1.at[n, 1, r, g - 1, at], on_x(g), self.hop1[h, r], self.source)

        def produce(self, columns, halfway=None, launch=True):
            for g in FAR_FIRST + (0,):
                if g == 3 and halfway:
                    halfway()
                there = turn(x, g)
                low = columns(pl.multiple_of(there * 512, 512)).astype(bf16)
                for c in range(4):
                    piece = low[:, c * W : (c + 1) * W]
                    self.part[0, there, c, pl.ds(0, H)] = piece[:H]
                    at = self.rows(1, False)
                    self.part[1, there, c, at] = piece[H : H + at.size]
                if launch:
                    self.launch(g, (0, 1))

        def produce_late(self, columns):
            for g in FAR_FIRST + (0,):
                there = turn(x, g)
                low = columns(pl.multiple_of(there * 512, 512)).astype(bf16)
                for c in range(4):
                    self.part[1, there, c, self.rows(2, False)] = low[:, c * W : (c + 1) * W]
                self.launch(g, (2,))

        def ride(self, h, products):
            tile = rider_tile(jnp.sum(products.T, axis=0, keepdims=True))
            for c in range(4):
                spot = (0, turn(x, 2), c) if h == 0 else (1, c, turn(z, 2))
                self.part[*spot, pl.ds(H, Q)] = tile

        def step(self, h, r):
            n, part = self.n, self.part
            self.hop1[h, r].wait()
            half = min(h, 1)
            spot = (turn(x, r), z) if half == 0 else (x, turn(z, r))
            at = self.rows(h, False)
            total = part[half, *spot, at].astype(f32)
            for d in range(3):
                total += rs_r1[n, half, r, d, at].astype(f32)
            if r == 2 and self.rides(h):
                rider = part[half, *spot, pl.ds(H, Q)].astype(f32)
                for d in range(3):
                    rider += rs_r1[n, half, r, d, pl.ds(H, Q)].astype(f32)
                self.row[half] = jnp.sum(rider, axis=0, keepdims=True)
                tile = rider_tile(self.row[half])
                for k in range(3):
                    rs_s2[n, half, k, pl.ds(H, Q)] = tile
            if r:
                rs_s2[n, half, r - 1, at] = total.astype(bf16)
                at = self.rows(h, True)
                src, dst = rs_s2.at[n, half, r - 1, at], rs_r2.at[n, half, r - 1, at]
                send(src, dst, axis_of(half, 0)(r), self.hop2[h], self.source)
            else:
                self.own[h] = total

        def middle(self, between=()):
            order = ((0, 2), (0, 1), (1, 2), (0, 3), (1, 1), (1, 3), (0, 0), (1, 0))
            if self.late:
                order += ((2, 2), (2, 1), (2, 3), (2, 0))
            for i, (h, r) in enumerate(order):
                self.step(h, r)
                for work in between:
                    if work[0] == i:
                        for call in work[1:]:
                            call()

        def end(self):
            n, out, column = self.n, [], []
            for h in sorted(self.hop2):
                half, at = min(h, 1), self.rows(h, False)
                self.hop2[h].wait()
                total = self.own[h]
                for r in range(3):
                    total += rs_r2[n, half, r, at].astype(f32)
                out.append(total)
                if self.rides(h):
                    row = self.row[half]
                    for r in range(3):
                        row += jnp.sum(rs_r2[n, half, r, pl.ds(H, Q)].astype(f32), axis=0, keepdims=True)
                    column.append(jnp.broadcast_to(row, (H, H)).T)
            return jnp.concatenate(out, 0), (jnp.concatenate(column, 0) if column else None)

    def chunk(buf, c):
        return jnp.concatenate([buf[0, c // 4, c % 4, pl.ds(0, H)], buf[1, c // 4, c % 4, pl.ds(0, H)]], 0)

    def gain_row(k, c):
        return tok_g[0, c // 4, c % 4, pl.ds(H, Q)].astype(f32)[k : k + 1]

    def norm(buf, k, scale_ref, dst):
        total = jnp.zeros((T, W), f32)
        for c in range(16):
            v = chunk(buf, c).astype(f32)
            total += v * v
        scale = lax.rsqrt(jnp.sum(total, axis=1, keepdims=True) * (1.0 / D) + EPS)
        scale_ref[...] = jnp.broadcast_to(scale, (T, W))
        for c in range(16):
            v = chunk(buf, c).astype(f32)
            dst[:, c * W : (c + 1) * W] = (v * scale_ref[...] * gain_row(k, c)).astype(bf16)

    def dense(buf, dst):
        for c in range(16):
            dst[:, c * W : (c + 1) * W] = chunk(buf, c)

    def block_at(there, core_there):
        return pl.multiple_of(((there % 2) * 4 + (there // 2) * 2 + core_there) * 256, 256)

    class Columns:
        def __init__(self, i, array):
            self.i, self.array, self.blocks = i, array, blocks.at[i]

        def start(self):
            self.group, source = Group(), Group(sources)
            for there in range(4):
                src = self.array.at[:, pl.ds(block_at(there, 1 - core), 256)]
                send(src, self.blocks.at[there, pl.ds(T, T)], other, self.group, source)
                src = self.array.at[:, pl.ds(block_at(there, core), 256)]
                pltpu.make_async_copy(src, self.blocks.at[there, pl.ds(0, T)], copy_sems.at[8 + self.i]).start()

        def ready(self):
            if not self.group.done:
                wait_bytes(copy_sems.at[8 + self.i], self.group.size)
            self.group.wait()

    class WeightGrad:
        def __init__(self, columns, left, g, relay, into):
            self.columns, self.left = columns, left
            self.g, self.relay, self.into, rows = g, relay, into, left.shape[0]
            cut = rows // 32 * 16 + (16 if rows % 32 else 0)
            self.a, self.b = pl.ds(0, cut), pl.ds(cut, rows - cut)

        def start(self, left):
            mine, peer = self.left.at[:, pl.ds(0, T)], self.left.at[:, pl.ds(T, T)]
            mine[...] = left
            self.source, self.pair = Group(sources), Group()
            send(mine, peer, other, self.pair, self.source)

        def make(self, k):
            there = turn(y, k)
            self.g[there] = nn(self.left[...], self.columns.blocks[there]).astype(bf16)
            return there

        def ready(self):
            self.pair.wait()
            self.columns.ready()
            self.last = Group()

        def compute(self):
            self.ready()
            self.relayed = Group()
            far = self.make(2)
            send(self.g.at[far, self.a], self.relay.at[self.a], on_y(1), self.relayed, self.source)
            send(self.g.at[far, self.b], self.relay.at[self.b], on_y(-1), self.relayed, self.source)
            for k, at in ((1, self.b), (-1, self.a)):
                there = self.make(k)
                send(self.g.at[there, at], self.into.at[(1 - k) // 2, at], on_y(k), self.last, self.source)
            self.make(0)

        def pass_on(self):
            self.relayed.wait()
            for k, at in ((1, self.a), (-1, self.b)):
                there = turn(y, k)
                self.g[there, at] = (self.g[there, at].astype(f32) + self.relay[at].astype(f32)).astype(bf16)
                send(self.g.at[there, at], self.into.at[(1 - k) // 2, at], on_y(k), self.last, self.source)

        def end(self):
            self.last.wait()
            return self.g[y].astype(f32) + self.into[0].astype(f32) + self.into[1].astype(f32)

        def compute_direct(self):
            self.ready()
            for k in FAR_FIRST:
                there = self.make(k)
                send(self.g.at[there], self.into.at[k - 1], on_y(k), self.last, self.source)
            self.make(0)

        def end_direct(self):
            return self.end() + self.into[2].astype(f32)

    def transposed(value):
        tp[:, :C] = value
        return tp[...].T[:C]

    columns_cot, columns_second, columns_gm, columns_first = [
        Columns(i, array) for i, array in enumerate((cot_d, second, gm_d, first))
    ]

    def weight_grad(columns, i, rows):
        refs = (left_mlp, g_mlp, relay_mlp, y_mlp) if rows == F else (left_rec, g_rec, relay_rec, y_rec)
        return WeightGrad(columns, *[ref.at[i] for ref in refs])

    down, up = weight_grad(columns_cot, 0, F), [weight_grad(columns_second, 1 + k, F) for k in range(2)]
    out, branches = weight_grad(columns_gm, 0, C), [weight_grad(columns_first, 1 + k, C) for k in range(2)]

    gain_tile = jnp.concatenate([gains[...].astype(f32), jnp.zeros((Q - 2, W), f32)], 0).astype(bf16)
    tok_g[0, x, z, pl.ds(H, Q)] = gain_tile
    load_tokens.wait()
    load_cot.wait()
    for h in range(2):
        tok_g[h, x, z, pl.ds(0, H)] = tokens[pl.ds(h * H, H)]
        cot_g[h, x, z] = cot[pl.ds(h * H, H)]
    tp[...] = jnp.zeros_like(tp)
    pl.semaphore_wait(barrier, len(partners))
    tok_gather = Gather(tok_g, (H + Q, H))
    tok_gather.forward()
    cot_gather = Gather(cot_g, (H, H))

    place_here = lax.broadcasted_iota(jnp.int32, (T, 1), 0) + seq * T
    start, begins = 0, [0]
    for j in range(3):
        start = start + lengths[0, j]
        begins.append(start)

    def begin_at(p):
        hit = p == begins[0]
        for b in begins[1:]:
            hit = jnp.logical_or(hit, p == b)
        return hit

    not_reset = jnp.where(begin_at(place_here), 0.0, 1.0)
    masks = [not_reset]
    for k in (1, 2):
        masks.append(masks[-1] * jnp.where(begin_at(place_here - k), 0.0, 1.0))

    tok_gather.end()
    norm(tok_g, 0, scale1, first)
    columns_first.start()
    for copy in load_branch + [load_gates]:
        copy.wait()

    value = nt(first[...], w_branch[pl.ds(CP, CP)])[:, :C]
    p1[...] = value
    inner = value.astype(bf16).astype(f32)
    ext[pl.ds(8, T)] = inner
    halo_s[:, :C] = inner[T - 8 :]
    halo = send_one(halo_s, halo_r, on_seq(1))
    cot_gather.forward()
    value = nt(first[...], w_branch[pl.ds(0, CP)])[:, :C]
    p0[...] = value
    act, slope = gelu_both(value)
    gel[...] = act
    dgel[...] = slope
    halo.wait()
    ext[pl.ds(0, 8)] = halo_r[:, :C]
    total = bias[0:1] + conv_w[0:1] * ext[pl.ds(8, T)]
    for k in (1, 2, 3):
        total = total + conv_w[k : k + 1] * (masks[k - 1] * ext[pl.ds(8 - k, T)])
    conv[...] = total
    conv_low = total.astype(bf16)
    rate = jax.nn.softplus(decay[...])
    r_gate = sigmoid(nn(conv_low, gates[0, 0]) + bias[1:2])
    rr[...] = r_gate
    a = jnp.exp(-8.0 * r_gate * rate)
    aa[...] = a
    coef[...] = a * not_reset
    i_gate = sigmoid(nn(conv_low, gates[1, 0]) + bias[2:3])
    ii[...] = i_gate
    root = jnp.sqrt(1.0 - a * a + 0.001)
    qq[...] = root

    def scan(A, B, reverse):
        step = 1
        while step < T:
            for ref, v, fill in ((pad_a, A, 1.0), (pad_b, B, 0.0)):
                ref[pl.ds(H, T)] = v
                ref[pl.ds(H + T if reverse else 0, H)] = jnp.full((H, C), fill, f32)
            at = pl.ds(H + step if reverse else H - step, T)
            B = B + A * pad_b[at]
            A = A * pad_a[at]
            step *= 2
        return A, B

    A, B = scan(coef[...], root * i_gate * conv[...], False)
    through[...] = A
    local[...] = B
    car_s[0:1, :C] = A[T - 1 :]
    car_s[1:2, :C] = B[T - 1 :]
    carries = Group()
    for d in (2, 1, 3):
        send(car_s, car_r.at[d - 1], on_seq(d), carries, misc)
    for copy in [load_out, load_down] + load_up:
        copy.wait()
    carries.wait()

    def fold(got, reverse):
        carried = jnp.zeros((1, C), f32)
        for d in (3, 2, 1):
            here = (seq + d < 4) if reverse else (seq - d >= 0)
            slot = 4 - d if reverse else d
            new = got[slot - 1, 0:1, :C] * carried + got[slot - 1, 1:2, :C]
            carried = jnp.where(here, new, carried)
        return carried

    carried = fold(car_r, False)
    value = local[...] + through[...] * carried
    state[...] = value
    prev[pl.ds(8, T)] = value
    prev[7:8] = carried
    mixed = gel[...] * value
    lhs[:, :C] = mixed.astype(bf16)
    scatter = Scatter(0, part1)
    scatter.produce(lambda at: nn(lhs[:, :CP], w_out[:, pl.ds(at, 512)]))
    o_states[...] = value[T - 1 :]
    mixed_t = transposed(mixed).astype(bf16)
    cot_gather.end()
    dense(cot_g, cot_d)
    columns_cot.start()

    scatter.middle()
    ghid[...] = nt(cot_d[...], w_down[...])
    branch, _ = scatter.end()
    middle = tokens[...].astype(f32) + branch
    mid_own[...] = middle
    middle_low = middle.astype(bf16)
    for h in range(2):
        mid_g[h, x, z] = middle_low[h * H : (h + 1) * H]
    gather = Gather(mid_g, (H, H))
    gather.forward()
    gather.end()
    norm(mid_g, 1, scale2, second)

    pair = nn(second[...], w_up[...])
    pair0, pair1 = pair[:, :F], pair[:, F:]
    act, slope = gelu_both(pair0)
    hidden = act * pair1
    gh = ghid[...]
    gp0 = slope * pair1 * gh
    gp1 = act * gh
    products = gp0 * pair0 + gp1 * pair1
    products = products[:, :W] + products[:, W : 2 * W] + products[:, 2 * W :]
    gp_low = jnp.concatenate([gp0.astype(bf16), gp1.astype(bf16)], 1)
    scatter = Scatter(1, part2, True)
    for h in range(2):
        scatter.ride(h, products[h * H : (h + 1) * H])

    down.start(hidden.T.astype(bf16))

    def halfway():
        up[0].start(gp0.T.astype(bf16))
        columns_second.start()
        up[1].start(gp1.T.astype(bf16))

    scatter.produce(lambda at: nt(gp_low, w_up[pl.ds(at, 512)]), halfway)
    down.compute()
    up[0].compute()
    scatter.middle(((3, up[1].compute), (7, down.pass_on)))

    grad_n, q = scatter.end()
    v = mid_own[...].astype(bf16).astype(f32)
    s = scale2[...]
    gain = gains[1:2].astype(f32)
    grad_middle_own = cot[...].astype(f32) + s * gain * grad_n - v * s * s * q * (1.0 / D)
    gmid_own[...] = grad_middle_own
    low = grad_middle_own.astype(bf16)
    for h in range(2):
        gm_g[h, x, z] = low[h * H : (h + 1) * H]
    gather = Gather(gm_g, (H, H))
    mine = small.at[dp * 4 + seq]
    mine[...] = jnp.zeros((16, 256), f32)
    mine[1:2, :W] = jnp.sum(grad_n * v * s, axis=0, keepdims=True)
    gather.forward()
    up[0].pass_on()
    hidden_low = hidden.astype(bf16)
    scatter_out = Scatter(2, part3)
    scatter_out.produce(lambda at: nn(hidden_low, w_down[:, pl.ds(at, 512)]), launch=False)
    up[1].pass_on()
    gather.end()
    for g in FAR_FIRST + (0,):
        scatter_out.launch(g, (0, 1))
    dense(gm_g, gm_d)
    columns_gm.start()

    grad_mixed = nt(gm_d[...], w_out[...])[:, :C]
    grad_y = dgel[...] * state[...] * grad_mixed
    grad_state = gel[...] * grad_mixed
    pad_a[pl.ds(0, T)] = coef[...]
    pad_a[pl.ds(T, 8)] = jnp.ones((8, C), f32)
    A, B = scan(pad_a[pl.ds(1, T)], grad_state, True)
    rev_s[0:1, :C] = through[T - 1 :]
    rev_s[1:2, :C] = coef[0:1] * B[0:1]
    carries = Group()
    for d in (2, 1, 3):
        send(rev_s, rev_r.at[d - 1], on_seq(d), carries, misc)
    out.start(mixed_t)
    branches[0].start(transposed(grad_y).astype(bf16))
    out.compute()
    branches[0].compute()
    cv_t = transposed(conv[...]).astype(bf16)
    carries.wait()
    total = B + A * fold(rev_r, True)
    a, r_gate, i_gate, root, cv = aa[...], rr[...], ii[...], qq[...], conv[...]
    t_i = total * i_gate
    d_log = total * prev[pl.ds(7, T)] * coef[...] - t_i * cv * (a * a / root)
    d_gate = d_log * r_gate
    mine[9:10, :C] = -8.0 * sigmoid(decay[...]) * jnp.sum(d_gate, axis=0, keepdims=True)
    gpre0 = -8.0 * rate * d_gate * (1.0 - r_gate)
    direct = t_i * root
    gpre1 = direct * cv * (1.0 - i_gate)
    low0, low1 = gpre0.astype(bf16), gpre1.astype(bf16)
    mine[7:8, :C] = jnp.sum(low0.astype(f32), axis=0, keepdims=True)
    mine[8:9, :C] = jnp.sum(low1.astype(f32), axis=0, keepdims=True)
    grad_conv = direct + nt(low0, gates[0, 0]) + nt(low1, gates[1, 0])
    mine[6:7, :C] = jnp.sum(grad_conv, axis=0, keepdims=True)
    edge = jnp.zeros((8, C), f32)
    grad_inner = jnp.zeros((T, C), f32)
    for k in range(4):
        weighted = grad_conv if k == 0 else masks[k - 1] * grad_conv
        mine[2 + k : 3 + k, :C] = jnp.sum(weighted * ext[pl.ds(8 - k, T)], axis=0, keepdims=True)
        if k == 0:
            pad_a[pl.ds(0, 8)] = jnp.zeros((8, C), f32)
            pad_a[pl.ds(8 + T, 8)] = jnp.zeros((8, C), f32)
        pad_a[pl.ds(8, T)] = conv_w[k : k + 1] * weighted
        edge += pad_a[pl.ds(k, 8)]
        grad_inner += pad_a[pl.ds(8 + k, T)]
    back_s[:, :C] = edge
    back = send_one(back_s, back_r, on_seq(-1))
    lhs[:, :C] = grad_y.astype(bf16)
    lhs[:, CP : CP + C] = grad_inner.astype(bf16)
    scatter = Scatter(3, part4, True, True)
    tp[:, :C] = grad_y * p0[...] + grad_inner * p1[...]
    scatter.ride(0, tp[pl.ds(0, H), :W] + tp[pl.ds(0, H), W:])

    scatter.produce(lambda at: nn(lhs[...], w_branch[:, pl.ds(at, 512)]))
    gg[0, :, :C] = nn(cv_t, low0).astype(bf16)
    gg[1, :, :C] = nn(cv_t, low1).astype(bf16)
    gg_pair = send_one(gg.at[1 - core], gg_r, other)
    gg_all = Group()
    mine = small.at[dp * 4 + seq]
    others = ((2, False), (2, True), (1, False), (1, True), (3, False), (3, True), (0, False))
    smalls, gain_sums = Group(), Group()
    for d, same in others:
        send(mine, mine, on_y(d, same), smalls, misc)
    out.pass_on()
    branches[0].pass_on()
    back.wait()
    ext[pl.ds(0, T)] = grad_inner
    ext[pl.ds(T - 8, 8)] = grad_inner[T - 8 :] + back_r[:, :C]
    grad_inner = ext[pl.ds(0, T)]
    tp[:, :C] = grad_y * p0[...] + grad_inner * p1[...]
    scatter.ride(1, tp[pl.ds(H, H), :W] + tp[pl.ds(H, H), W:])
    late = pl.ds(T - LATE, LATE)
    lhs[late, CP : CP + C] = grad_inner[T - LATE :].astype(bf16)
    scatter.produce_late(lambda at: nn(lhs[late], w_branch[:, pl.ds(at, 512)]))
    branches[1].start(transposed(grad_inner).astype(bf16))
    def gates_middle():
        gg_pair.wait()
        gg_y[y] = (gg[core].astype(f32) + gg_r[...].astype(f32)).astype(bf16)
        for d in FAR_FIRST:
            send(gg_y.at[y], gg_y.at[y], on_y(d), gg_all, misc)

    scatter.middle((
        (0, gates_middle), (1, branches[1].compute_direct),
    ))
    scatter_out.middle()
    o_down[...] = down.end()
    for k in range(2):
        o_up[k] = up[k].end().T

    grad_n, q = scatter.end()
    v = tokens[...].astype(f32)
    s = scale1[...]
    gain = gains[0:1].astype(f32)
    mine = gain_one.at[dp * 4 + seq]
    mine[...] = jnp.broadcast_to(jnp.sum(grad_n * v * s, axis=0, keepdims=True), (8, W))
    for d, same in others:
        send(mine, mine, on_y(d, same), gain_sums, misc)
    gg_all.wait()
    gg_f[core] = gg_y[0].astype(f32) + gg_y[1].astype(f32) + gg_y[2].astype(f32) + gg_y[3].astype(f32)
    gg_share = send_one(gg_f.at[core], gg_f.at[core], other)
    o_tokens[...] = gmid_own[...] + s * gain * grad_n - v * s * s * q * (1.0 / D)
    o_out[...] = out.end()
    result, _ = scatter_out.end()
    o_block[...] = (mid_own[...] + result).astype(bf16)
    o_branch[0] = branches[0].end()
    o_branch[1] = branches[1].end_direct()
    gg_share.wait()
    for k in range(2):
        o_gates[k, 0] = gg_f[k, :, :C]
    smalls.wait()
    total = small[0]
    for j in range(1, 8):
        total += small[j]
    o_gains[1:2] = total[1:2, :W]
    o_conv[...] = total[2:6, :C]
    o_bias[...] = total[6:9, :C]
    o_decay[...] = total[9:10, :C]
    gain_sums.wait()
    total = gain_one[0, 0:1]
    for j in range(1, 8):
        total += gain_one[j, 0:1]
    o_gains[0:1] = total
    finish()


def hand_over(*refs):
    n = 12
    copies = [pltpu.make_async_copy(refs[i], refs[n + i], refs[-1].at[i]) for i in range(n)]
    for copy in copies:
        copy.start()
    for copy in copies:
        copy.wait()


def on_device(
    tokens, doc_lengths, cotangent, norm_gains, w_branch, conv_weight, lru_bias, decay, gate_weights, w_out, w_up, w_down
):
    def shape(dims, kind=f32):
        return jax.ShapeDtypeStruct(dims, kind)

    def vmem(*dims):
        return pltpu.VMEM(dims, f32)

    def low(*dims):
        return pltpu.VMEM(dims, bf16)

    near, far = pl.BlockSpec(memory_space=pltpu.VMEM), pl.BlockSpec(memory_space=pl.ANY)
    outs = [
        shape((T, W), bf16), shape((T, W)), shape((2, W)), shape((2, C, 256)), shape((4, C)), shape((3, C)),
        shape((1, C)), shape((2, 1, C, C)), shape((C, 256)), shape((2, 256, F)), shape((F, 256)), shape((1, C)),
    ]
    scratch = (
        [low(T, W), low(T, W), low(2 * CP, D), low(2, 1, C, C), low(CP, D), low(D, 2 * F), low(F, D)]
        + [low(2, 4, 4, H + Q, W)] + [low(2, 4, 4, H, W)] * 3 + [low(T, D)] * 4
        + [low(2, 4, 4, H + Q, W)] * 4
        + [low(4, 2, 4, 3, H + Q, W), low(4, 2, 3, H + Q, W), low(4, 2, 3, H + Q, W)]
        + [vmem(T + 8, C)] + [vmem(T, C)] * 13 + [vmem(T + 8, C), vmem(2 * H + T, C), vmem(2 * H + T, C), vmem(T, T)]
        + [vmem(T, F), vmem(T, W), vmem(T, W), vmem(T, W), vmem(T, W)]
        + [low(4, 4, 2 * T, 256)]
        + [low(3, F, 2 * T), low(3, 4, F, 256), low(3, F, 256), low(3, 2, F, 256)]
        + [low(3, C, 2 * T), low(3, 4, C, 256), low(3, C, 256), low(3, 3, C, 256), low(T, 2 * CP)]
        + [vmem(8, 256)] * 4 + [vmem(8, 256), vmem(3, 8, 256)] * 2
        + [low(2, C, 256), low(C, 256), low(4, C, 256), vmem(2, C, 256)]
        + [vmem(8, 16, 256), vmem(8, 8, W), vmem(6144, W)]
        + [pltpu.SemaphoreType.DMA((N_SENT,)), pltpu.SemaphoreType.DMA((N_SEMS,)), pltpu.SemaphoreType.DMA((12,))]
    )
    made = pl.pallas_call(
        kernel,
        out_shape=[pltpu.VMEM(o.shape, o.dtype) for o in outs],
        in_specs=[pl.BlockSpec(memory_space=pltpu.SMEM)] + [near] * 4 + [far] * 7,
        out_specs=[near] * 12,
        scratch_shapes=scratch,
        compiler_params=pltpu.CompilerParams(
            collective_id=0, has_side_effects=True, vmem_limit_bytes=56 * 2**20
        ),
    )(
        doc_lengths, norm_gains, conv_weight, lru_bias, decay.reshape(1, C), tokens.reshape(T, W),
        cotangent.reshape(T, W), jnp.swapaxes(w_branch, 1, 2), gate_weights, w_out, w_up, w_down,
    )
    made = list(pl.pallas_call(
        hand_over,
        out_shape=outs,
        in_specs=[near] * 12,
        out_specs=[far] * 12,
        scratch_shapes=[pltpu.SemaphoreType.DMA((12,))],
        compiler_params=pltpu.CompilerParams(vmem_limit_bytes=2 * 2**20),
    )(*made))
    made[0], made[1] = made[0].reshape(1, T, W), made[1].reshape(1, T, W)
    made[3] = jnp.swapaxes(made[3], 1, 2)
    made[6], made[11] = made[6].reshape(C), made[11].reshape(1, 1, C)
    return tuple(made)


def solution(mesh):
    in_specs = (
        P("dp", "seq", "mp"), P("dp", None), P("dp", "seq", "mp"), P(None, "mp"), P(None, None, "mp"), P(None, "mp"),
        P(None, "mp"), P("mp"), P(None, "mp", None, None), P("mp", None), P(None, None, "mp"), P("mp", None),
    )
    out_specs = (
        P("dp", "seq", "mp"), P("dp", "seq", "mp"), P(None, "mp"), P(None, ("dp", "seq"), "mp"), P(None, "mp"),
        P(None, "mp"), P("mp"), P(None, "mp", None, None), P("mp", ("dp", "seq")), P(None, ("dp", "seq"), "mp"),
        P("mp", ("dp", "seq")), P("dp", "seq", "mp"),
    )
    return jax.shard_map(on_device, mesh=mesh, in_specs=in_specs, out_specs=out_specs, check_vma=False)
```

time: 103 us -> 96.6 us (0.938)
  Pallas kernels: 102 us -> 95.6 us
    pallas_call x2, Pallas kernels: 102 us -> 95.6 us  [the longest x1 94.1 us: on_device(): pl.pallas_call(kernel, out_shape=[pltpu.VMEM(o.shape, o.dtype) for o in o...]
where the time goes in v3:
time: 96.6 us; the launch traced here: 96.4 us
  Pallas kernels  95.6 us (99%)
    pallas_call x1, Pallas kernels, on_device(): pl.pallas_call(kernel, out_shape=[pltpu.VMEM(o.shape, o.dtype) for o in o...  94.1 us

profile of v3, /device:TPU:1, one launch (start us, length us, event | category | flops | bytes accessed | tf_op | source)
XLA Modules:
  0.0 96.4 jit_solution(14563008537317572479)
XLA Ops:
  0.6 94.1 %shard_map.211 = (bf16[256,128]{1,0:T(8,128)(2,1)S(1)}, f32[256,128]{1,0:T(8,128)S(1)}, f32[2,128]{1,0:T(2,128)S(1)}, f32[2,176,256]{2,1,0:T(8,128)S(1)}, f32[4,...) custom-call(s32[1,4]{1,0:T(1,128)} %lengths.1, ...), custom_call_target="tpu_custom_call" | custom-call | tf_op jit(solution)/shard_map/pallas_call | solution.py:743
  94.8 1.5 %shard_map.212 = (bf16[256,128]{1,0:T(8,128)(2,1)}, f32[256,128]{1,0:T(8,128)}, f32[2,128]{1,0:T(2,128)}, f32[2,176,256]{2,1,0:T(8,128)}, f32[4,176]{1,0:T(4,128...) custom-call(bf16[256,128]{1,0:T(8,128)(2,1)S(1)} %get-tuple-element., ...), custom_call_target="tpu_custom_call" | custom-call | tf_op jit(solution)/shard_map/pallas_call | solution.py:756

commit v4 on v3

--- a/solution.py
+++ b/solution.py
@@ -10,8 +10,9 @@
 
 T, D, C, F, W = 256, 2048, 176, 384, 128
 H = T // 2
+S = T // 4
 EPS = 1e-06
-N_SEMS, N_SENT = 112, 28
+N_SEMS, N_SENT = 152, 24
 CP = 256
 LATE = 16
 Q = 16
@@ -39,8 +40,10 @@
 
 
 def rider_tile(row):
+    if row.shape[1] < W:
+        row = jnp.concatenate([row, jnp.zeros((1, W - row.shape[1]), f32)], 1)
     high = row.astype(bf16).astype(f32)
-    index = lax.broadcasted_iota(jnp.int32, (Q, H), 0)
+    index = lax.broadcasted_iota(jnp.int32, (Q, W), 0)
     return jnp.where(index == 0, high, jnp.where(index == 1, row - high, 0.0)).astype(bf16)
 
 
@@ -48,13 +51,13 @@
     lengths, gains, conv_w, bias, decay, hbm_tokens, hbm_cot, hbm_branch, hbm_gates, hbm_out, hbm_up, hbm_down,
     o_block, o_tokens, o_gains, o_branch, o_conv, o_bias, o_decay, o_gates, o_out, o_up, o_down, o_states,
     tokens, cot, w_branch, gates, w_out, w_up, w_down,
-    tok_g, cot_g, mid_g, gm_g, first, second, cot_d, gm_d,
-    part1, part2, part3, part4, rs_r1, rs_s2, rs_r2,
+    tok_g, cot_g, mid_g, gm_g, tok_v, cot_v, mid_v, gm_v, first, second, cot_d, gm_d,
+    part_s, r1_s, s2_s, r2_s, part_b, r1_b, s2_b, r2_b, hidden_low, grad_y_s, grad_state_s,
     ext, conv, aa, rr, ii, qq, coef, through, local, p0, p1, gel, dgel, state, prev, pad_a, pad_b, tp,
     ghid, mid_own, gmid_own, scale1, scale2,
     blocks, left_mlp, g_mlp, relay_mlp, y_mlp, left_rec, g_rec, relay_rec, y_rec, lhs,
     halo_s, halo_r, back_s, back_r, car_s, car_r, rev_s, rev_r,
-    gg, gg_r, gg_y, gg_f, small, gain_one, ruler,
+    gg, gg_r, gg_y, gg_f, small_own, small_mate, small, gain_one, ruler,
     send_sems, recv_sems, copy_sems,
 ):
     me, seq, dp = lax.axis_index("mp"), lax.axis_index("seq"), lax.axis_index("dp")
@@ -64,11 +67,13 @@
     def turn(value, by):
         return lax.rem(value + by + 4, 4)
 
+    mate = (seq // 2) * 2 + (1 - core)
+
     def on_x(d):
-        return {"mp": turn(x, d) * 4 + z}
+        return {"mp": turn(x, d) * 4 + z, "seq": mate}
 
     def on_z(d):
-        return {"mp": x * 4 + turn(z, d)}
+        return {"mp": x * 4 + turn(z, d), "seq": mate}
 
     def on_y(d, same=True):
         there = turn(y, d)
@@ -144,69 +149,70 @@
     def axis_of(h, phase):
         return (on_x, on_z)[(h + phase) % 2]
 
-    def place(h, first_hop, second_hop):
-        return (turn(x, first_hop), turn(z, second_hop)) if h == 0 else (turn(x, second_hop), turn(z, first_hop))
+    def place(h, first_hop):
+        return (turn(x, first_hop), z) if h == 0 else (x, turn(z, first_hop))
 
     class Gather:
-        def __init__(self, buf, rows):
-            self.buf, self.rows = buf, rows
-            self.arrivals, self.source = [], Group(sources)
-            for d in (1, 3, 2):
+        def __init__(self, buf, via, rows):
+            self.buf, self.via, self.rows = buf, via, rows
+            self.arrivals, self.last, self.source = [], Group(), Group(sources)
+            for d in (1, 3, 2, 0):
                 for h in range(2):
-                    ref, group = self.view(h, x, z), Group()
-                    send(ref, ref, axis_of(h, 0)(d), group, self.source)
+                    group = Group()
+                    send(self.view(buf, h, 0), self.view(via, h, 0), axis_of(h, 0)(d), group, self.source)
                     self.arrivals.append((h, d, group))
-            self.last = Group()
-            for h in range(2):
-                self.pass_on(h, 0)
-
-        def view(self, h, cx, cz):
-            return self.buf.at[h, cx, cz, pl.ds(0, self.rows[h])]
-
-        def pass_on(self, h, d):
-            ref = self.view(h, *place(h, -d, 0))
-            for e in (1, 3, 2):
-                send(ref, ref, axis_of(h, 1)(e), self.last, self.source)
+
+        def view(self, buf, h, d):
+            return buf.at[h, *place(h, -d), pl.ds(0, self.rows[h])]
 
         def forward(self):
-            for h, d, group in self.arrivals:
+            for h, d, group in self.arrivals[-2:] + self.arrivals[:-2]:
                 group.wait()
-                self.pass_on(h, d)
+                src, dst = self.view(self.via, h, d), self.view(self.buf, h, d)
+                for e in (1, 3, 2):
+                    send(src, dst, axis_of(h, 1)(e), self.last, self.source)
+                if d:
+                    send(src, dst, other, self.last, self.source)
 
         def end(self):
             self.last.wait()
 
     class Scatter:
-        def __init__(self, n, part, rider=False, late=False):
-            self.n, self.part, self.rider, self.late = n, part, rider, late
+        def __init__(self, refs, rider=False, late=False):
+            self.part, self.r1, self.s2, self.r2 = refs
+            self.size = self.part.shape[3] - Q
+            self.rider, self.late = rider, late
             self.source = Group(sources)
             self.hop1 = {(h, r): Group() for h in range(2) for r in range(4)}
             self.hop2 = {h: Group() for h in range(2)}
             if late:
                 self.hop1.update({(2, r): Group() for r in range(4)})
                 self.hop2[2] = Group()
-            self.own, self.row = {}, {}
 
         def rows(self, h, rider):
-            first, size = ((0, H), (0, H - LATE if self.late else H), (H - LATE, LATE))[h]
+            first, size = ((0, self.size), (0, self.size - LATE if self.late else self.size), (self.size - LATE, LATE))[h]
             return pl.ds(first, size + (Q if rider and self.rides(h) else 0))
 
         def rides(self, h):
             return self.rider and h in ((0, 2) if self.late else (0, 1))
 
         def launch(self, g, halves):
-            n, part = self.n, self.part
             for h in halves:
-                if h == 0:
-                    for d in FAR_FIRST:
-                        at = self.rows(h, g == 2)
-                        src = part.at[0, turn(x, g), turn(z, d), at]
-                        send(src, rs_r1.at[n, 0, g, d - 1, at], on_z(d), self.hop1[0, g], self.source)
-                elif g:
-                    for r in FAR_FIRST + (0,):
-                        at = self.rows(h, r == 2)
-                        src = part.at[1, turn(x, g), turn(z, r), at]
-                        send(src, rs_r1.at[n, 1, r, g - 1, at], on_x(g), self.hop1[h, r], self.source)
+                for k in FAR_FIRST + (0,):
+                    if h == 0 or k:
+                        r, d = (g, k) if h == 0 else (k, g)
+                        self.pass_part(h, r, d)
+            if g == 0 and not (self.late and 0 in halves):
+                for h in (1, 2) if self.late else (1,):
+                    for k in FAR_FIRST + (0,):
+                        self.pass_part(h, 0, k)
+
+        def pass_part(self, h, r, d):
+            half = min(h, 1)
+            spot = (turn(x, r), turn(z, d)) if half == 0 else (turn(x, d), turn(z, r))
+            at = self.rows(h, r == 2)
+            src, dst = self.part.at[half, *spot, at], self.r1.at[half, r, d, at]
+            send(src, dst, axis_of(half, 1)(d), self.hop1[h, r], self.source)
 
         def produce(self, columns, halfway=None, launch=True):
             for g in FAR_FIRST + (0,):
@@ -216,11 +222,12 @@
                 low = columns(pl.multiple_of(there * 512, 512)).astype(bf16)
                 for c in range(4):
                     piece = low[:, c * W : (c + 1) * W]
-                    self.part[0, there, c, pl.ds(0, H)] = piece[:H]
+                    self.part[0, there, c, pl.ds(0, self.size)] = piece[: self.size]
                     at = self.rows(1, False)
-                    self.part[1, there, c, at] = piece[H : H + at.size]
-                if launch:
-                    self.launch(g, (0, 1))
+                    self.part[1, there, c, at] = piece[self.size : self.size + at.size]
+                if launch and g in (1, 0):
+                    for k in (2, 1) if g == 1 else (3, 0):
+                        self.launch(k, (0, 1))
 
         def produce_late(self, columns):
             for g in FAR_FIRST + (0,):
@@ -234,37 +241,30 @@
             tile = rider_tile(jnp.sum(products.T, axis=0, keepdims=True))
             for c in range(4):
                 spot = (0, turn(x, 2), c) if h == 0 else (1, c, turn(z, 2))
-                self.part[*spot, pl.ds(H, Q)] = tile
+                self.part[*spot, pl.ds(self.size, Q)] = tile
 
         def step(self, h, r):
-            n, part = self.n, self.part
+            half, extra = min(h, 1), pl.ds(self.size, Q)
             self.hop1[h, r].wait()
-            half = min(h, 1)
-            spot = (turn(x, r), z) if half == 0 else (x, turn(z, r))
+
+            def total(at):
+                parts = [self.r1[half, r, d, at].astype(f32) for d in range(4)]
+                return (parts[0] + parts[1]) + (parts[2] + parts[3])
+
+            if r == 2 and self.rides(h):
+                tile = rider_tile(jnp.sum(total(extra), axis=0, keepdims=True))
+                for k in range(4):
+                    self.s2[half, k, extra] = tile
             at = self.rows(h, False)
-            total = part[half, *spot, at].astype(f32)
-            for d in range(3):
-                total += rs_r1[n, half, r, d, at].astype(f32)
-            if r == 2 and self.rides(h):
-                rider = part[half, *spot, pl.ds(H, Q)].astype(f32)
-                for d in range(3):
-                    rider += rs_r1[n, half, r, d, pl.ds(H, Q)].astype(f32)
-                self.row[half] = jnp.sum(rider, axis=0, keepdims=True)
-                tile = rider_tile(self.row[half])
-                for k in range(3):
-                    rs_s2[n, half, k, pl.ds(H, Q)] = tile
-            if r:
-                rs_s2[n, half, r - 1, at] = total.astype(bf16)
-                at = self.rows(h, True)
-                src, dst = rs_s2.at[n, half, r - 1, at], rs_r2.at[n, half, r - 1, at]
-                send(src, dst, axis_of(half, 0)(r), self.hop2[h], self.source)
-            else:
-                self.own[h] = total
+            self.s2[half, r, at] = total(at).astype(bf16)
+            at = self.rows(h, True)
+            send(self.s2.at[half, r, at], self.r2.at[half, r, at], axis_of(half, 0)(r), self.hop2[h], self.source)
 
         def middle(self, between=()):
-            order = ((0, 2), (0, 1), (1, 2), (0, 3), (1, 1), (1, 3), (0, 0), (1, 0))
+            order = ((0, 2), (0, 1), (1, 2), (0, 3), (1, 1), (1, 3))
             if self.late:
                 order += ((2, 2), (2, 1), (2, 3), (2, 0))
+            order += ((0, 0), (1, 0))
             for i, (h, r) in enumerate(order):
                 self.step(h, r)
                 for work in between:
@@ -273,41 +273,44 @@
                             call()
 
         def end(self):
-            n, out, column = self.n, [], []
+            out, column = [], []
             for h in sorted(self.hop2):
                 half, at = min(h, 1), self.rows(h, False)
                 self.hop2[h].wait()
-                total = self.own[h]
-                for r in range(3):
-                    total += rs_r2[n, half, r, at].astype(f32)
-                out.append(total)
+                parts = [self.r2[half, r, at].astype(f32) for r in range(4)]
+                out.append((parts[0] + parts[1]) + (parts[2] + parts[3]))
                 if self.rides(h):
-                    row = self.row[half]
-                    for r in range(3):
-                        row += jnp.sum(rs_r2[n, half, r, pl.ds(H, Q)].astype(f32), axis=0, keepdims=True)
-                    column.append(jnp.broadcast_to(row, (H, H)).T)
+                    rider = self.r2[half, 0, pl.ds(self.size, Q)].astype(f32)
+                    for r in range(1, 4):
+                        rider += self.r2[half, r, pl.ds(self.size, Q)].astype(f32)
+                    row = jnp.sum(rider, axis=0, keepdims=True)
+                    column.append(jnp.broadcast_to(row, (W, W)).T[: self.size])
             return jnp.concatenate(out, 0), (jnp.concatenate(column, 0) if column else None)
 
     def chunk(buf, c):
-        return jnp.concatenate([buf[0, c // 4, c % 4, pl.ds(0, H)], buf[1, c // 4, c % 4, pl.ds(0, H)]], 0)
+        size = min(buf.shape[3], H)
+        return jnp.concatenate([buf[h, c // 4, c % 4, pl.ds(0, size)] for h in range(2)], 0)
 
     def gain_row(k, c):
         return tok_g[0, c // 4, c % 4, pl.ds(H, Q)].astype(f32)[k : k + 1]
 
-    def norm(buf, k, scale_ref, dst):
-        total = jnp.zeros((T, W), f32)
+    def norm(buf, k, at):
+        scale_ref, dst = ((scale1, first), (scale2, second))[k]
+        total = jnp.zeros((at.size, W), f32)
         for c in range(16):
             v = chunk(buf, c).astype(f32)
             total += v * v
         scale = lax.rsqrt(jnp.sum(total, axis=1, keepdims=True) * (1.0 / D) + EPS)
-        scale_ref[...] = jnp.broadcast_to(scale, (T, W))
+        scale_ref[at] = jnp.broadcast_to(scale, (at.size, W))
         for c in range(16):
             v = chunk(buf, c).astype(f32)
-            dst[:, c * W : (c + 1) * W] = (v * scale_ref[...] * gain_row(k, c)).astype(bf16)
-
-    def dense(buf, dst):
+            dst[at, c * W : (c + 1) * W] = (v * scale_ref[at] * gain_row(k, c)).astype(bf16)
+
+    def dense(buf, dst, at):
         for c in range(16):
-            dst[:, c * W : (c + 1) * W] = chunk(buf, c)
+            dst[at, c * W : (c + 1) * W] = chunk(buf, c)
+
+    everything, streams = pl.ds(0, T), [pl.ds(0, H), pl.ds(H, H)]
 
     def block_at(there, core_there):
         return pl.multiple_of(((there % 2) * 4 + (there // 2) * 2 + core_there) * 256, 256)
@@ -336,32 +339,29 @@
             cut = rows // 32 * 16 + (16 if rows % 32 else 0)
             self.a, self.b = pl.ds(0, cut), pl.ds(cut, rows - cut)
 
-        def start(self, left):
+        def start(self, left=None):
             mine, peer = self.left.at[:, pl.ds(0, T)], self.left.at[:, pl.ds(T, T)]
-            mine[...] = left
+            if left is not None:
+                mine[...] = left
             self.source, self.pair = Group(sources), Group()
             send(mine, peer, other, self.pair, self.source)
 
-        def make(self, k):
-            there = turn(y, k)
-            self.g[there] = nn(self.left[...], self.columns.blocks[there]).astype(bf16)
-            return there
-
-        def ready(self):
+        def make(self):
             self.pair.wait()
             self.columns.ready()
             self.last = Group()
+            for there in range(4):
+                self.g[there] = nn(self.left[...], self.columns.blocks[there]).astype(bf16)
 
         def compute(self):
-            self.ready()
+            self.make()
             self.relayed = Group()
-            far = self.make(2)
+            far = turn(y, 2)
             send(self.g.at[far, self.a], self.relay.at[self.a], on_y(1), self.relayed, self.source)
             send(self.g.at[far, self.b], self.relay.at[self.b], on_y(-1), self.relayed, self.source)
             for k, at in ((1, self.b), (-1, self.a)):
-                there = self.make(k)
-                send(self.g.at[there, at], self.into.at[(1 - k) // 2, at], on_y(k), self.last, self.source)
-            self.make(0)
+                src = self.g.at[turn(y, k), at]
+                send(src, self.into.at[(1 - k) // 2, at], on_y(k), self.last, self.source)
 
         def pass_on(self):
             self.relayed.wait()
@@ -375,11 +375,9 @@
             return self.g[y].astype(f32) + self.into[0].astype(f32) + self.into[1].astype(f32)
 
         def compute_direct(self):
-            self.ready()
+            self.make()
             for k in FAR_FIRST:
-                there = self.make(k)
-                send(self.g.at[there], self.into.at[k - 1], on_y(k), self.last, self.source)
-            self.make(0)
+                send(self.g.at[turn(y, k)], self.into.at[k - 1], on_y(k), self.last, self.source)
 
         def end_direct(self):
             return self.end() + self.into[2].astype(f32)
@@ -408,9 +406,9 @@
         cot_g[h, x, z] = cot[pl.ds(h * H, H)]
     tp[...] = jnp.zeros_like(tp)
     pl.semaphore_wait(barrier, len(partners))
-    tok_gather = Gather(tok_g, (H + Q, H))
+    tok_gather = Gather(tok_g, tok_v, (H + Q, H))
     tok_gather.forward()
-    cot_gather = Gather(cot_g, (H, H))
+    cot_gather = Gather(cot_g, cot_v, (H, H))
 
     place_here = lax.broadcasted_iota(jnp.int32, (T, 1), 0) + seq * T
     start, begins = 0, [0]
@@ -430,7 +428,7 @@
         masks.append(masks[-1] * jnp.where(begin_at(place_here - k), 0.0, 1.0))
 
     tok_gather.end()
-    norm(tok_g, 0, scale1, first)
+    norm(tok_g, 0, everything)
     columns_first.start()
     for copy in load_branch + [load_gates]:
         copy.wait()
@@ -505,81 +503,99 @@
     prev[7:8] = carried
     mixed = gel[...] * value
     lhs[:, :C] = mixed.astype(bf16)
-    scatter = Scatter(0, part1)
-    scatter.produce(lambda at: nn(lhs[:, :CP], w_out[:, pl.ds(at, 512)]))
+
+    def stream_refs(i):
+        return [ref.at[i] for ref in (part_s, r1_s, s2_s, r2_s)]
+
+    def part_refs(i):
+        return [ref.at[i] for ref in (part_b, r1_b, s2_b, r2_b)]
+
+    sums = [Scatter(stream_refs(i)) for i in range(2)]
+    for at, scatter in zip(streams, sums):
+        scatter.produce(lambda c: nn(lhs[at, :CP], w_out[:, pl.ds(c, 512)]))
     o_states[...] = value[T - 1 :]
     mixed_t = transposed(mixed).astype(bf16)
     cot_gather.end()
-    dense(cot_g, cot_d)
+    dense(cot_g, cot_d, everything)
+    sums[0].middle()
     columns_cot.start()
-
-    scatter.middle()
+    sums[1].middle()
+    gathers = []
+    for i, at in enumerate(streams):
+        branch, _ = sums[i].end()
+        middle = tokens[at].astype(f32) + branch
+        mid_own[at] = middle
+        middle_low = middle.astype(bf16)
+        for h in range(2):
+            mid_g[i, h, x, z] = middle_low[h * S : (h + 1) * S]
+        gathers.append(Gather(mid_g.at[i], mid_v.at[i], (S, S)))
+    gathers[0].forward()
     ghid[...] = nt(cot_d[...], w_down[...])
-    branch, _ = scatter.end()
-    middle = tokens[...].astype(f32) + branch
-    mid_own[...] = middle
-    middle_low = middle.astype(bf16)
-    for h in range(2):
-        mid_g[h, x, z] = middle_low[h * H : (h + 1) * H]
-    gather = Gather(mid_g, (H, H))
-    gather.forward()
-    gather.end()
-    norm(mid_g, 1, scale2, second)
-
-    pair = nn(second[...], w_up[...])
-    pair0, pair1 = pair[:, :F], pair[:, F:]
-    act, slope = gelu_both(pair0)
-    hidden = act * pair1
-    gh = ghid[...]
-    gp0 = slope * pair1 * gh
-    gp1 = act * gh
-    products = gp0 * pair0 + gp1 * pair1
-    products = products[:, :W] + products[:, W : 2 * W] + products[:, 2 * W :]
-    gp_low = jnp.concatenate([gp0.astype(bf16), gp1.astype(bf16)], 1)
-    scatter = Scatter(1, part2, True)
-    for h in range(2):
-        scatter.ride(h, products[h * H : (h + 1) * H])
-
-    down.start(hidden.T.astype(bf16))
-
-    def halfway():
-        up[0].start(gp0.T.astype(bf16))
-        columns_second.start()
-        up[1].start(gp1.T.astype(bf16))
-
-    scatter.produce(lambda at: nt(gp_low, w_up[pl.ds(at, 512)]), halfway)
+    gathers[1].forward()
+
+    sums = [Scatter(stream_refs(2 + i), True) for i in range(2)]
+    for i, at in enumerate(streams):
+        gathers[i].end()
+        norm(mid_g.at[i], 1, at)
+        pair = nn(second[at], w_up[...])
+        pair0, pair1 = pair[:, :F], pair[:, F:]
+        act, slope = gelu_both(pair0)
+        hidden = act * pair1
+        gh = ghid[at]
+        gp0 = slope * pair1 * gh
+        gp1 = act * gh
+        products = gp0 * pair0 + gp1 * pair1
+        products = products[:, :W] + products[:, W : 2 * W] + products[:, 2 * W :]
+        gp_low = jnp.concatenate([gp0.astype(bf16), gp1.astype(bf16)], 1)
+        for h in range(2):
+            sums[i].ride(h, products[h * S : (h + 1) * S])
+        sums[i].produce(lambda c: nt(gp_low, w_up[pl.ds(c, 512)]))
+        hidden_low[at] = hidden.astype(bf16)
+        for grad, left in ((down, hidden), (up[0], gp0), (up[1], gp1)):
+            grad.left[:, at] = left.T.astype(bf16)
+    down.start()
+    columns_second.start()
+    for grad in up:
+        grad.start()
+    sums[0].middle()
     down.compute()
+    sums[1].middle()
     up[0].compute()
-    scatter.middle(((3, up[1].compute), (7, down.pass_on)))
-
-    grad_n, q = scatter.end()
-    v = mid_own[...].astype(bf16).astype(f32)
-    s = scale2[...]
+
+    gathers, gain_sum = [], jnp.zeros((1, W), f32)
     gain = gains[1:2].astype(f32)
-    grad_middle_own = cot[...].astype(f32) + s * gain * grad_n - v * s * s * q * (1.0 / D)
-    gmid_own[...] = grad_middle_own
-    low = grad_middle_own.astype(bf16)
-    for h in range(2):
-        gm_g[h, x, z] = low[h * H : (h + 1) * H]
-    gather = Gather(gm_g, (H, H))
-    mine = small.at[dp * 4 + seq]
+    for i, at in enumerate(streams):
+        grad_n, q = sums[i].end()
+        v = mid_own[at].astype(bf16).astype(f32)
+        s = scale2[at]
+        grad_middle_own = cot[at].astype(f32) + s * gain * grad_n - v * s * s * q * (1.0 / D)
+        gmid_own[at] = grad_middle_own
+        low = grad_middle_own.astype(bf16)
+        for h in range(2):
+            gm_g[i, h, x, z] = low[h * S : (h + 1) * S]
+        gathers.append(Gather(gm_g.at[i], gm_v.at[i], (S, S)))
+        gain_sum += jnp.sum(grad_n * v * s, axis=0, keepdims=True)
+    mine = small_own
     mine[...] = jnp.zeros((16, 256), f32)
-    mine[1:2, :W] = jnp.sum(grad_n * v * s, axis=0, keepdims=True)
-    gather.forward()
+    mine[1:2, :W] = gain_sum
+    gathers[0].forward()
+    up[1].compute()
+    down.pass_on()
+    gathers[1].forward()
     up[0].pass_on()
-    hidden_low = hidden.astype(bf16)
-    scatter_out = Scatter(2, part3)
-    scatter_out.produce(lambda at: nn(hidden_low, w_down[:, pl.ds(at, 512)]), launch=False)
-    up[1].pass_on()
-    gather.end()
-    for g in FAR_FIRST + (0,):
-        scatter_out.launch(g, (0, 1))
-    dense(gm_g, gm_d)
-    columns_gm.start()
-
-    grad_mixed = nt(gm_d[...], w_out[...])[:, :C]
-    grad_y = dgel[...] * state[...] * grad_mixed
-    grad_state = gel[...] * grad_mixed
+    scatter_out = Scatter(part_refs(0))
+    scatter_out.produce(lambda c: nn(hidden_low[...], w_down[:, pl.ds(c, 512)]), launch=False)
+    for i, at in enumerate(streams):
+        gathers[i].end()
+        dense(gm_g.at[i], gm_d, at)
+        grad_mixed = nt(gm_d[at], w_out[...])[:, :C]
+        grad_y_s[at] = dgel[at] * state[at] * grad_mixed
+        grad_state_s[at] = gel[at] * grad_mixed
+        if i == 0:
+            for g in FAR_FIRST + (0,):
+                scatter_out.launch(g, (0, 1))
+    grad_y, grad_state = grad_y_s[...], grad_state_s[...]
+
     pad_a[pl.ds(0, T)] = coef[...]
     pad_a[pl.ds(T, 8)] = jnp.ones((8, C), f32)
     A, B = scan(pad_a[pl.ds(1, T)], grad_state, True)
@@ -588,6 +604,8 @@
     carries = Group()
     for d in (2, 1, 3):
         send(rev_s, rev_r.at[d - 1], on_seq(d), carries, misc)
+    columns_gm.start()
+    up[1].pass_on()
     out.start(mixed_t)
     branches[0].start(transposed(grad_y).astype(bf16))
     out.compute()
@@ -621,24 +639,22 @@
         grad_inner += pad_a[pl.ds(8 + k, T)]
     back_s[:, :C] = edge
     back = send_one(back_s, back_r, on_seq(-1))
-    lhs[:, :C] = grad_y.astype(bf16)
-    lhs[:, CP : CP + C] = grad_inner.astype(bf16)
-    scatter = Scatter(3, part4, True, True)
-    tp[:, :C] = grad_y * p0[...] + grad_inner * p1[...]
-    scatter.ride(0, tp[pl.ds(0, H), :W] + tp[pl.ds(0, H), W:])
-
-    scatter.produce(lambda at: nn(lhs[...], w_branch[:, pl.ds(at, 512)]))
     gg[0, :, :C] = nn(cv_t, low0).astype(bf16)
     gg[1, :, :C] = nn(cv_t, low1).astype(bf16)
     gg_pair = send_one(gg.at[1 - core], gg_r, other)
     gg_all = Group()
-    mine = small.at[dp * 4 + seq]
-    others = ((2, False), (2, True), (1, False), (1, True), (3, False), (3, True), (0, False))
-    smalls, gain_sums = Group(), Group()
-    for d, same in others:
-        send(mine, mine, on_y(d, same), smalls, misc)
-    out.pass_on()
-    branches[0].pass_on()
+    lhs[:, :C] = grad_y.astype(bf16)
+    lhs[:, CP : CP + C] = grad_inner.astype(bf16)
+    scatter = Scatter(part_refs(1), True, True)
+    tp[:, :C] = grad_y * p0[...] + grad_inner * p1[...]
+    scatter.ride(0, tp[pl.ds(0, H), :W] + tp[pl.ds(0, H), W:])
+
+    scatter.produce(lambda at: nn(lhs[...], w_branch[:, pl.ds(at, 512)]))
+    small_pair = send_one(small_own, small_mate, other)
+    gg_pair.wait()
+    gg_y[y] = (gg[core].astype(f32) + gg_r[...].astype(f32)).astype(bf16)
+    for d in FAR_FIRST:
+        send(gg_y.at[y], gg_y.at[y], on_y(d), gg_all, misc)
     back.wait()
     ext[pl.ds(0, T)] = grad_inner
     ext[pl.ds(T - 8, 8)] = grad_inner[T - 8 :] + back_r[:, :C]
@@ -649,19 +665,20 @@
     lhs[late, CP : CP + C] = grad_inner[T - LATE :].astype(bf16)
     scatter.produce_late(lambda at: nn(lhs[late], w_branch[:, pl.ds(at, 512)]))
     branches[1].start(transposed(grad_inner).astype(bf16))
-    def gates_middle():
-        gg_pair.wait()
-        gg_y[y] = (gg[core].astype(f32) + gg_r[...].astype(f32)).astype(bf16)
-        for d in FAR_FIRST:
-            send(gg_y.at[y], gg_y.at[y], on_y(d), gg_all, misc)
-
-    scatter.middle((
-        (0, gates_middle), (1, branches[1].compute_direct),
-    ))
+    others = ((2, False), (2, True), (1, False), (1, True), (3, False), (3, True), (0, False))
+    smalls, gain_sums = Group(), Group()
+    out.pass_on()
+    branches[0].pass_on()
+    small_pair.wait()
+    small[y] = small_own[...] + small_mate[...]
+    for d in FAR_FIRST:
+        send(small.at[y], small.at[y], on_y(d), smalls, misc)
+    scatter.middle(((1, branches[1].compute_direct),))
     scatter_out.middle()
     o_down[...] = down.end()
     for k in range(2):
         o_up[k] = up[k].end().T
+
 
     grad_n, q = scatter.end()
     v = tokens[...].astype(f32)
@@ -685,7 +702,7 @@
         o_gates[k, 0] = gg_f[k, :, :C]
     smalls.wait()
     total = small[0]
-    for j in range(1, 8):
+    for j in range(1, 4):
         total += small[j]
     o_gains[1:2] = total[1:2, :W]
     o_conv[...] = total[2:6, :C]
@@ -727,9 +744,10 @@
     ]
     scratch = (
         [low(T, W), low(T, W), low(2 * CP, D), low(2, 1, C, C), low(CP, D), low(D, 2 * F), low(F, D)]
-        + [low(2, 4, 4, H + Q, W)] + [low(2, 4, 4, H, W)] * 3 + [low(T, D)] * 4
-        + [low(2, 4, 4, H + Q, W)] * 4
-        + [low(4, 2, 4, 3, H + Q, W), low(4, 2, 3, H + Q, W), low(4, 2, 3, H + Q, W)]
+        + ([low(2, 4, 4, H + Q, W), low(2, 4, 4, H, W)] + [low(2, 2, 4, 4, S, W)] * 2) * 2 + [low(T, D)] * 4
+        + [low(4, 2, 4, 4, S + Q, W)] * 2 + [low(4, 2, 4, S + Q, W)] * 2
+        + [low(2, 2, 4, 4, H + Q, W)] * 2 + [low(2, 2, 4, H + Q, W)] * 2
+        + [low(T, F), vmem(T, C), vmem(T, C)]
         + [vmem(T + 8, C)] + [vmem(T, C)] * 13 + [vmem(T + 8, C), vmem(2 * H + T, C), vmem(2 * H + T, C), vmem(T, T)]
         + [vmem(T, F), vmem(T, W), vmem(T, W), vmem(T, W), vmem(T, W)]
         + [low(4, 4, 2 * T, 256)]
@@ -737,7 +755,7 @@
         + [low(3, C, 2 * T), low(3, 4, C, 256), low(3, C, 256), low(3, 3, C, 256), low(T, 2 * CP)]
         + [vmem(8, 256)] * 4 + [vmem(8, 256), vmem(3, 8, 256)] * 2
         + [low(2, C, 256), low(C, 256), low(4, C, 256), vmem(2, C, 256)]
-        + [vmem(8, 16, 256), vmem(8, 8, W), vmem(6144, W)]
+        + [vmem(16, 256), vmem(16, 256), vmem(4, 16, 256), vmem(8, 8, W), vmem(6144, W)]
         + [pltpu.SemaphoreType.DMA((N_SENT,)), pltpu.SemaphoreType.DMA((N_SEMS,)), pltpu.SemaphoreType.DMA((12,))]
     )
     made = pl.pallas_call(

time: 96.6 us -> 94.8 us (0.981)
  Pallas kernels: 95.6 us -> 93.9 us
    pallas_call x1, Pallas kernels: 94.1 us -> 92.4 us  [on_device(): pl.pallas_call(kernel, out_shape=[pltpu.VMEM(o.shape, o.dtype) for o in o...]
where the time goes in v4:
time: 94.8 us; the launch traced here: 94.7 us
  Pallas kernels  93.9 us (99%)
    pallas_call x1, Pallas kernels, on_device(): pl.pallas_call(kernel, out_shape=[pltpu.VMEM(o.shape, o.dtype) for o in o...  92.4 us

profile of v4, /device:TPU:1, one launch (start us, length us, event | category | flops | bytes accessed | tf_op | source)
XLA Modules:
  0.0 94.7 jit_solution(17229744933054460898)
XLA Ops:
  0.6 92.4 %shard_map.211 = (bf16[256,128]{1,0:T(8,128)(2,1)S(1)}, f32[256,128]{1,0:T(8,128)S(1)}, f32[2,128]{1,0:T(2,128)S(1)}, f32[2,176,256]{2,1,0:T(8,128)S(1)}, f32[4,...) custom-call(s32[1,4]{1,0:T(1,128)} %lengths.1, ...), custom_call_target="tpu_custom_call" | custom-call | tf_op jit(solution)/shard_map/pallas_call | solution.py:761
  93.0 1.5 %shard_map.212 = (bf16[256,128]{1,0:T(8,128)(2,1)}, f32[256,128]{1,0:T(8,128)}, f32[2,128]{1,0:T(2,128)}, f32[2,176,256]{2,1,0:T(8,128)}, f32[4,176]{1,0:T(4,128...) custom-call(bf16[256,128]{1,0:T(8,128)(2,1)S(1)} %get-tuple-element., ...), custom_call_target="tpu_custom_call" | custom-call | tf_op jit(solution)/shard_map/pallas_call | solution.py:774

commit v5 on v4

--- a/solution.py
+++ b/solution.py
@@ -12,7 +12,7 @@
 H = T // 2
 S = T // 4
 EPS = 1e-06
-N_SEMS, N_SENT = 152, 24
+N_SEMS, N_SENT = 160, 24
 CP = 256
 LATE = 16
 Q = 16
@@ -216,7 +216,7 @@
 
         def produce(self, columns, halfway=None, launch=True):
             for g in FAR_FIRST + (0,):
-                if g == 3 and halfway:
+                if g == 1 and halfway:
                     halfway()
                 there = turn(x, g)
                 low = columns(pl.multiple_of(there * 512, 512)).astype(bf16)
@@ -225,8 +225,8 @@
                     self.part[0, there, c, pl.ds(0, self.size)] = piece[: self.size]
                     at = self.rows(1, False)
                     self.part[1, there, c, at] = piece[self.size : self.size + at.size]
-                if launch and g in (1, 0):
-                    for k in (2, 1) if g == 1 else (3, 0):
+                if launch and g in (2, 0):
+                    for k in (2,) if g == 2 else (1, 3, 0):
                         self.launch(k, (0, 1))
 
         def produce_late(self, columns):
@@ -287,28 +287,27 @@
                     column.append(jnp.broadcast_to(row, (W, W)).T[: self.size])
             return jnp.concatenate(out, 0), (jnp.concatenate(column, 0) if column else None)
 
-    def chunk(buf, c):
-        size = min(buf.shape[3], H)
+    def chunk(buf, c, size):
         return jnp.concatenate([buf[h, c // 4, c % 4, pl.ds(0, size)] for h in range(2)], 0)
 
     def gain_row(k, c):
-        return tok_g[0, c // 4, c % 4, pl.ds(H, Q)].astype(f32)[k : k + 1]
+        return tok_g[1, 0, c // 4, c % 4, pl.ds(S, Q)].astype(f32)[k : k + 1]
 
     def norm(buf, k, at):
         scale_ref, dst = ((scale1, first), (scale2, second))[k]
         total = jnp.zeros((at.size, W), f32)
         for c in range(16):
-            v = chunk(buf, c).astype(f32)
+            v = chunk(buf, c, at.size // 2).astype(f32)
             total += v * v
         scale = lax.rsqrt(jnp.sum(total, axis=1, keepdims=True) * (1.0 / D) + EPS)
         scale_ref[at] = jnp.broadcast_to(scale, (at.size, W))
         for c in range(16):
-            v = chunk(buf, c).astype(f32)
+            v = chunk(buf, c, at.size // 2).astype(f32)
             dst[at, c * W : (c + 1) * W] = (v * scale_ref[at] * gain_row(k, c)).astype(bf16)
 
     def dense(buf, dst, at):
         for c in range(16):
-            dst[at, c * W : (c + 1) * W] = chunk(buf, c)
+            dst[at, c * W : (c + 1) * W] = chunk(buf, c, at.size // 2)
 
     everything, streams = pl.ds(0, T), [pl.ds(0, H), pl.ds(H, H)]
 
@@ -398,16 +397,18 @@
     out, branches = weight_grad(columns_gm, 0, C), [weight_grad(columns_first, 1 + k, C) for k in range(2)]
 
     gain_tile = jnp.concatenate([gains[...].astype(f32), jnp.zeros((Q - 2, W), f32)], 0).astype(bf16)
-    tok_g[0, x, z, pl.ds(H, Q)] = gain_tile
+    tok_g[1, 0, x, z, pl.ds(S, Q)] = gain_tile
     load_tokens.wait()
     load_cot.wait()
     for h in range(2):
-        tok_g[h, x, z, pl.ds(0, H)] = tokens[pl.ds(h * H, H)]
+        for i in range(2):
+            tok_g[i, h, x, z, pl.ds(0, S)] = tokens[pl.ds(i * H + h * S, S)]
         cot_g[h, x, z] = cot[pl.ds(h * H, H)]
     tp[...] = jnp.zeros_like(tp)
     pl.semaphore_wait(barrier, len(partners))
-    tok_gather = Gather(tok_g, tok_v, (H + Q, H))
-    tok_gather.forward()
+    tok_gathers = {i: Gather(tok_g.at[i], tok_v.at[i], (S + Q if i else S, S)) for i in (1, 0)}
+    for i in (1, 0):
+        tok_gathers[i].forward()
     cot_gather = Gather(cot_g, cot_v, (H, H))
 
     place_here = lax.broadcasted_iota(jnp.int32, (T, 1), 0) + seq * T
@@ -427,24 +428,22 @@
     for k in (1, 2):
         masks.append(masks[-1] * jnp.where(begin_at(place_here - k), 0.0, 1.0))
 
-    tok_gather.end()
-    norm(tok_g, 0, everything)
+    for i in (1, 0):
+        tok_gathers[i].end()
+        at = streams[i]
+        norm(tok_g.at[i], 0, at)
+        if i:
+            for copy in load_branch + [load_gates]:
+                copy.wait()
+        value = nt(first[at], w_branch[pl.ds(CP, CP)])[:, :C]
+        p1[at] = value
+        inner = value.astype(bf16).astype(f32)
+        ext[pl.ds(8 + i * H, H)] = inner
+        if i:
+            halo_s[:, :C] = inner[H - 8 :]
+            halo = send_one(halo_s, halo_r, on_seq(1))
+    cot_gather.forward()
     columns_first.start()
-    for copy in load_branch + [load_gates]:
-        copy.wait()
-
-    value = nt(first[...], w_branch[pl.ds(CP, CP)])[:, :C]
-    p1[...] = value
-    inner = value.astype(bf16).astype(f32)
-    ext[pl.ds(8, T)] = inner
-    halo_s[:, :C] = inner[T - 8 :]
-    halo = send_one(halo_s, halo_r, on_seq(1))
-    cot_gather.forward()
-    value = nt(first[...], w_branch[pl.ds(0, CP)])[:, :C]
-    p0[...] = value
-    act, slope = gelu_both(value)
-    gel[...] = act
-    dgel[...] = slope
     halo.wait()
     ext[pl.ds(0, 8)] = halo_r[:, :C]
     total = bias[0:1] + conv_w[0:1] * ext[pl.ds(8, T)]
@@ -483,6 +482,11 @@
     carries = Group()
     for d in (2, 1, 3):
         send(car_s, car_r.at[d - 1], on_seq(d), carries, misc)
+    value = nt(first[...], w_branch[pl.ds(0, CP)])[:, :C]
+    p0[...] = value
+    act, slope = gelu_both(value)
+    gel[...] = act
+    dgel[...] = slope
     for copy in [load_out, load_down] + load_up:
         copy.wait()
     carries.wait()
@@ -639,19 +643,22 @@
         grad_inner += pad_a[pl.ds(8 + k, T)]
     back_s[:, :C] = edge
     back = send_one(back_s, back_r, on_seq(-1))
-    gg[0, :, :C] = nn(cv_t, low0).astype(bf16)
-    gg[1, :, :C] = nn(cv_t, low1).astype(bf16)
-    gg_pair = send_one(gg.at[1 - core], gg_r, other)
-    gg_all = Group()
     lhs[:, :C] = grad_y.astype(bf16)
     lhs[:, CP : CP + C] = grad_inner.astype(bf16)
     scatter = Scatter(part_refs(1), True, True)
     tp[:, :C] = grad_y * p0[...] + grad_inner * p1[...]
     scatter.ride(0, tp[pl.ds(0, H), :W] + tp[pl.ds(0, H), W:])
 
-    scatter.produce(lambda at: nn(lhs[...], w_branch[:, pl.ds(at, 512)]))
+    gg_pairs, gg_all = [], Group()
+
+    def gates_grad():
+        gg[0, :, :C] = nn(cv_t, low0).astype(bf16)
+        gg[1, :, :C] = nn(cv_t, low1).astype(bf16)
+        gg_pairs.append(send_one(gg.at[1 - core], gg_r, other))
+
+    scatter.produce(lambda at: nn(lhs[...], w_branch[:, pl.ds(at, 512)]), gates_grad)
     small_pair = send_one(small_own, small_mate, other)
-    gg_pair.wait()
+    gg_pairs[0].wait()
     gg_y[y] = (gg[core].astype(f32) + gg_r[...].astype(f32)).astype(bf16)
     for d in FAR_FIRST:
         send(gg_y.at[y], gg_y.at[y], on_y(d), gg_all, misc)
@@ -673,7 +680,7 @@
     small[y] = small_own[...] + small_mate[...]
     for d in FAR_FIRST:
         send(small.at[y], small.at[y], on_y(d), smalls, misc)
-    scatter.middle(((1, branches[1].compute_direct),))
+    scatter.middle(((3, branches[1].compute_direct),))
     scatter_out.middle()
     o_down[...] = down.end()
     for k in range(2):
@@ -744,7 +751,7 @@
     ]
     scratch = (
         [low(T, W), low(T, W), low(2 * CP, D), low(2, 1, C, C), low(CP, D), low(D, 2 * F), low(F, D)]
-        + ([low(2, 4, 4, H + Q, W), low(2, 4, 4, H, W)] + [low(2, 2, 4, 4, S, W)] * 2) * 2 + [low(T, D)] * 4
+        + ([low(2, 2, 4, 4, S + Q, W), low(2, 4, 4, H, W)] + [low(2, 2, 4, 4, S, W)] * 2) * 2 + [low(T, D)] * 4
         + [low(4, 2, 4, 4, S + Q, W)] * 2 + [low(4, 2, 4, S + Q, W)] * 2
         + [low(2, 2, 4, 4, H + Q, W)] * 2 + [low(2, 2, 4, H + Q, W)] * 2
         + [low(T, F), vmem(T, C), vmem(T, C)]
@@ -755,7 +762,7 @@
         + [low(3, C, 2 * T), low(3, 4, C, 256), low(3, C, 256), low(3, 3, C, 256), low(T, 2 * CP)]
         + [vmem(8, 256)] * 4 + [vmem(8, 256), vmem(3, 8, 256)] * 2
         + [low(2, C, 256), low(C, 256), low(4, C, 256), vmem(2, C, 256)]
-        + [vmem(16, 256), vmem(16, 256), vmem(4, 16, 256), vmem(8, 8, W), vmem(6144, W)]
+        + [vmem(16, 256), vmem(16, 256), vmem(4, 16, 256), vmem(8, 8, W), vmem(3072, W)]
         + [pltpu.SemaphoreType.DMA((N_SENT,)), pltpu.SemaphoreType.DMA((N_SEMS,)), pltpu.SemaphoreType.DMA((12,))]
     )
     made = pl.pallas_call(

time: 94.8 us -> 93.1 us (0.982)
  Pallas kernels: 93.9 us -> 92.1 us
    pallas_call x1, Pallas kernels: 92.4 us -> 90.6 us  [on_device(): pl.pallas_call(kernel, out_shape=[pltpu.VMEM(o.shape, o.dtype) for o in o...]
where the time goes in v5:
time: 93.1 us; the launch traced here: 92.9 us
  Pallas kernels  92.1 us (99%)
    pallas_call x1, Pallas kernels, on_device(): pl.pallas_call(kernel, out_shape=[pltpu.VMEM(o.shape, o.dtype) for o in o...  90.6 us

profile of v5, /device:TPU:1, one launch (start us, length us, event | category | flops | bytes accessed | tf_op | source)
XLA Modules:
  0.0 92.9 jit_solution(9641861620134648533)
XLA Ops:
  0.6 90.6 %shard_map.211 = (bf16[256,128]{1,0:T(8,128)(2,1)S(1)}, f32[256,128]{1,0:T(8,128)S(1)}, f32[2,128]{1,0:T(2,128)S(1)}, f32[2,176,256]{2,1,0:T(8,128)S(1)}, f32[4,...) custom-call(s32[1,4]{1,0:T(1,128)} %lengths.1, ...), custom_call_target="tpu_custom_call" | custom-call | tf_op jit(solution)/shard_map/pallas_call | solution.py:768
  91.3 1.5 %shard_map.212 = (bf16[256,128]{1,0:T(8,128)(2,1)}, f32[256,128]{1,0:T(8,128)}, f32[2,128]{1,0:T(2,128)}, f32[2,176,256]{2,1,0:T(8,128)}, f32[4,176]{1,0:T(4,128...) custom-call(bf16[256,128]{1,0:T(8,128)(2,1)S(1)} %get-tuple-element., ...), custom_call_target="tpu_custom_call" | custom-call | tf_op jit(solution)/shard_map/pallas_call | solution.py:781

commit v6 on v5

--- a/solution.py
+++ b/solution.py
@@ -12,7 +12,7 @@
 H = T // 2
 S = T // 4
 EPS = 1e-06
-N_SEMS, N_SENT = 160, 24
+N_SEMS, N_SENT = 126, 24
 CP = 256
 LATE = 16
 Q = 16
@@ -157,8 +157,8 @@
             self.buf, self.via, self.rows = buf, via, rows
             self.arrivals, self.last, self.source = [], Group(), Group(sources)
             for d in (1, 3, 2, 0):
+                group = Group()
                 for h in range(2):
-                    group = Group()
                     send(self.view(buf, h, 0), self.view(via, h, 0), axis_of(h, 0)(d), group, self.source)
                     self.arrivals.append((h, d, group))
 
@@ -184,7 +184,7 @@
             self.rider, self.late = rider, late
             self.source = Group(sources)
             self.hop1 = {(h, r): Group() for h in range(2) for r in range(4)}
-            self.hop2 = {h: Group() for h in range(2)}
+            self.hop2 = dict.fromkeys(range(2), Group())
             if late:
                 self.hop1.update({(2, r): Group() for r in range(4)})
                 self.hop2[2] = Group()

time: 93.1 us -> 92.7 us (level)
  no operation moved by 1% of the time
where the time goes in v6:
time: 92.7 us; the launch traced here: 92.6 us
  Pallas kernels  91.7 us (99%)
    pallas_call x1, Pallas kernels, on_device(): pl.pallas_call(kernel, out_shape=[pltpu.VMEM(o.shape, o.dtype) for o in o...  90.2 us

profile of v6, /device:TPU:1, one launch (start us, length us, event | category | flops | bytes accessed | tf_op | source)
XLA Modules:
  0.0 92.6 jit_solution(2313540197970019146)
XLA Ops:
  0.6 90.2 %shard_map.211 = (bf16[256,128]{1,0:T(8,128)(2,1)S(1)}, f32[256,128]{1,0:T(8,128)S(1)}, f32[2,128]{1,0:T(2,128)S(1)}, f32[2,176,256]{2,1,0:T(8,128)S(1)}, f32[4,...) custom-call(s32[1,4]{1,0:T(1,128)} %lengths.1, ...), custom_call_target="tpu_custom_call" | custom-call | tf_op jit(solution)/shard_map/pallas_call | solution.py:768
  90.9 1.5 %shard_map.212 = (bf16[256,128]{1,0:T(8,128)(2,1)}, f32[256,128]{1,0:T(8,128)}, f32[2,128]{1,0:T(2,128)}, f32[2,176,256]{2,1,0:T(8,128)}, f32[4,176]{1,0:T(4,128...) custom-call(bf16[256,128]{1,0:T(8,128)(2,1)S(1)} %get-tuple-element., ...), custom_call_target="tpu_custom_call" | custom-call | tf_op jit(solution)/shard_map/pallas_call | solution.py:781
